TPU v7x, 512 devices: a whole 4x4x16 slice. The times are simulated.
512 devices in a mesh: sect: 4 (over y), seq: 128 (over z, x, core).
Axes of the slice: x: 4, y: 4, z: 16, core: 2. Of those that a mesh axis runs over, the one named last changes fastest.
Arguments:
- tokens: bfloat16 [1024, 6144], P('seq'), may hold values from -6 to 6
- routes: int32 [1024, 2], P('seq'), may hold values from 0 to 7, all different within a row; in each aligned block of 8 rows (0 to 7, 8 to 15, ...) at most 3 rows name the same one
- w_router: bfloat16 [6144, 8], replicated, may hold values from -0.078125 to 0.078125
- w_gate: bfloat16 [6144, 65536], P(None, ('seq', 'sect')), may hold values from -0.078125 to 0.078125
- w_up: bfloat16 [6144, 65536], P(None, ('seq', 'sect')), may hold values from -0.078125 to 0.078125
- cotangent: bfloat16 [384, 65536], P(None, ('seq', 'sect')), may hold values from -6 to 6
Outputs:
- hidden: bfloat16 [384, 65536], P(None, ('seq', 'sect'))
- grad_tokens: bfloat16 [1024, 6144], P('seq')
- grad_router: float32 [6144, 8], replicated
Inputs may be any that keep to these rules, and one draw needn't show every extreme that they name: `routes`: the two experts of a token differ. Among the tokens of one index of seq (aligned blocks of 8 tokens) no expert is named more than 3 times, and in every draw some block names some expert exactly 3 times.
All inputs are finite; a program needn't handle non-finite values.
Results may differ from a plain program's by a relative error of at most 0.0055.
Values may be sent and summed in bfloat16 or wider, within the bound.
No kernel may reach another device: no remote copies, remote signals or barrier semaphores. Data moves between devices by JAX's collectives and lax.ppermute only.
A program may use at most 128 MiB of HBM per device.

v0:
```python
import jax
import jax.numpy as jnp
from jax import lax
from jax.sharding import PartitionSpec as P

highest = lax.Precision.HIGHEST


def slot_select(routes, experts, most):
    pairs = routes.reshape(-1)
    onehot = (pairs[:, None] == jnp.arange(experts, dtype=jnp.int32)[None, :]).astype(jnp.int32)
    ranks = jnp.sum((jnp.cumsum(onehot, axis=0) - 1) * onehot, axis=1)
    places = pairs * most + ranks
    return (places[None, :] == jnp.arange(experts * most, dtype=jnp.int32)[:, None]).astype(
        jnp.float32
    )


def local(tokens, routes, w_router, w_gate, w_up, cotangent):
    tok_rows, width = tokens.shape
    experts = w_router.shape[1]
    seq_count = lax.axis_size("seq")
    slots = cotangent.shape[0]
    most = slots // seq_count
    group = seq_count // experts
    logits = jnp.dot(tokens, w_router, preferred_element_type=jnp.float32)
    choose = (routes[:, :, None] == jnp.arange(experts, dtype=jnp.int32)[None, None, :]).astype(
        jnp.float32
    )
    picked = jnp.sum(choose * logits[:, None, :], axis=2)
    probs = jax.nn.softmax(picked, axis=1)
    select = slot_select(routes, experts, most)
    pair_rows = jnp.repeat(tokens, 2, axis=0)
    buffer = jnp.dot(
        select.astype(jnp.bfloat16), pair_rows, preferred_element_type=jnp.float32
    ).astype(jnp.bfloat16)
    weight_slots = jnp.dot(select, probs.reshape(-1), precision=highest)
    outgoing = jnp.repeat(buffer.reshape(experts, most, width), group, axis=0).reshape(
        seq_count * most, width
    )
    out_weights = (
        jnp.repeat(weight_slots.reshape(experts, most), group, axis=0)
        .reshape(-1)
        .astype(jnp.bfloat16)
    )
    rows, slot_weight = (
        lax.all_to_all(outgoing, "seq", split_axis=0, concat_axis=0, tiled=True),
        lax.all_to_all(out_weights, "seq", split_axis=0, concat_axis=0, tiled=True),
    )
    gate_pre = jnp.dot(rows, w_gate, preferred_element_type=jnp.float32)
    up_pre = jnp.dot(rows, w_up, preferred_element_type=jnp.float32)
    weight_col = slot_weight.astype(jnp.float32)[:, None]
    sigma = jax.nn.sigmoid(gate_pre)
    act = gate_pre * sigma * up_pre
    hidden = (weight_col * act).astype(jnp.bfloat16)
    grad_out = cotangent.astype(jnp.float32)
    slot_dp = jnp.sum(grad_out * act, axis=1)
    d_gate = (grad_out * weight_col * up_pre * sigma * (1.0 + gate_pre * (1.0 - sigma))).astype(
        jnp.bfloat16
    )
    d_up = (grad_out * weight_col * gate_pre * sigma).astype(jnp.bfloat16)
    dims = (((1,), (1,)), ((), ()))
    slot_dx = lax.dot_general(d_gate, w_gate, dims, preferred_element_type=jnp.float32)
    slot_dx = slot_dx + lax.dot_general(d_up, w_up, dims, preferred_element_type=jnp.float32)
    back_dx, back_dp = (
        lax.all_to_all(slot_dx, "seq", split_axis=0, concat_axis=0, tiled=True),
        lax.all_to_all(slot_dp, "seq", split_axis=0, concat_axis=0, tiled=True),
    )
    summed_dx = (
        back_dx.reshape(experts, group, most, width).sum(axis=1).reshape(experts * most, width)
    )
    summed_dp = back_dp.reshape(experts, group, most).sum(axis=1).reshape(experts * most)
    pair_dx = jnp.dot(select.T, summed_dx, precision=highest)
    token_dx = pair_dx.reshape(tok_rows, 2, width).sum(axis=1)
    pair_dp = jnp.dot(select.T, summed_dp, precision=highest).reshape(tok_rows, 2)
    token_dx, pair_dp = lax.psum((token_dx, pair_dp), "sect")
    mean_dp = jnp.sum(probs * pair_dp, axis=1, keepdims=True)
    d_pick = probs * (pair_dp - mean_dp)
    d_logits = jnp.sum(choose * d_pick[:, :, None], axis=1)
    router_dx = jnp.dot(d_logits, w_router.astype(jnp.float32).T, precision=highest)
    grad_tokens = (token_dx + router_dx).astype(jnp.bfloat16)
    router_part = jnp.dot(tokens.astype(jnp.float32).T, d_logits, precision=highest)
    grad_router = lax.psum(router_part, "seq")
    return (hidden, grad_tokens, grad_router)


def solution(mesh):
    placed = (
        P("seq", None),
        P("seq", None),
        P(),
        P(None, ("seq", "sect")),
        P(None, ("seq", "sect")),
        P(None, ("seq", "sect")),
    )
    return jax.shard_map(
        local,
        mesh=mesh,
        in_specs=placed,
        out_specs=(P(None, ("seq", "sect")), P("seq", None), P()),
        check_vma=False,
    )
```

profile of v0, /device:TPU:1, one launch (start us, length us, event | category | flops | bytes accessed | tf_op | source)
XLA Modules:
  0.0 1367.4 jit_solution(7040284964163833876)
XLA Ops:
  7.2 1.1 broadcast_in_dim.7
  9.9 5.8 broadcast_in_dim.8
  15.7 20.9 %all-to-all-start.1 = ((bf16[128,3,6144]{2,1,0:T(4,128)(2,1)}), bf16[128,3,6144]{2,1,0:T(4,128)(2,1)}, u32[]{:S(2)}, u32[]{:S(2)}) async-start(bf16[128,3,6144]{2,1,0:T(4,128)(2,1)} %bitcast.35), calls=%async_computation.1 | async-start | bytes 12582912 | tf_op jit(solution)/shard_map/all_to_all | solution.py:47
  38.5 272.5 %all-to-all-done.1 = bf16[128,3,6144]{2,1,0:T(4,128)(2,1)} async-done(((bf16[128,3,6144]{2,1,0:T(4,128)(2,1)}), bf16[128,3,6144]{2,1,0:T(4,128)(2,1)}, u32[]{:S(2)}, u32[]{:S(2)}) %all-to-all-start.1) | async-done | bytes 4718624 | tf_op jit(solution)/shard_map/all_to_all | solution.py:47
  311.0 12.4 all_to_all.27
  323.4 3.9 fusion.32
  327.3 1.5 fusion.8
  328.8 0.8 all_to_all.30
  329.7 12.7 all-to-all-start.3
  342.4 1.2 fusion.27
  343.7 13.2 all-to-all-done.3
  356.9 0.9 reduce_sum.90
  358.4 1.5 fusion.20
  359.9 8.8 psum.22
  368.8 1.2 multiply_reduce_fusion
  370.6 0.8 fusion.16
  371.7 0.8 copy.43
  372.5 23.0 %all_to_all.36 = bf16[128,3,1]{1,2,0:T(2,128)(2,1)S(1)} all-to-all(bf16[128,3,1]{1,2,0:T(2,128)(2,1)} %copy.43), channel_id=1, replica_groups=mesh['sect'=4,'seq'=128] {'seq'}, dimensions={0} | all-to-all | bytes 1536 | tf_op jit(solution)/shard_map/all_to_all | solution.py:48
  395.4 0.8 convert_reduce_fusion
  396.2 1.0 reshape.149
  397.3 2.4 fusion.10
  399.7 5.0 convolution_add_fusion
  404.7 14.5 %all_to_all.28 = f32[128,3,6144]{2,1,0:T(4,128)} reshape(f32[384,6144]{1,0:T(8,128)} %convolution_add_fusion) | data formatting | bytes 18874368 | tf_op jit(solution)/shard_map/all_to_all | solution.py:66
  419.2 7.0 all-to-all-start.2
  426.4 544.8 %all-to-all-done.2 = f32[128,3,6144]{2,1,0:T(4,128)} async-done(((f32[128,3,6144]{2,1,0:T(4,128)}), f32[128,3,6144]{2,1,0:T(4,128)}, u32[]{:S(2)}, u32[]{:S(2)}) %all-to-all-start.2) | async-done | bytes 9437216 | tf_op jit(solution)/shard_map/all_to_all | solution.py:66
  971.2 6.6 bitcast_reduce_fusion
  978.1 1.1 convolution_reduce_fusion
  979.3 1.0 convolution_bitcast_fusion
  981.1 47.2 %all-reduce.3.cloned.1.call-done = f32[8,6144]{1,0:T(8,128)} async-done(((f32[8,6144]{1,0:T(8,128)}), f32[8,6144]{1,0:T(8,128)}) %all-reduce.3.cloned.1.call-update) | async-done | bytes 196624 | tf_op jit(solution)/shard_map/psum | solution.py:76
  1028.3 1.8 fusion
  1030.1 328.8 %all-reduce.5.cloned.1.call-done = f32[6144,8]{0,1:T(8,128)} async-done(((f32[6144,8]{0,1:T(8,128)}), f32[6144,8]{0,1:T(8,128)}) %all-reduce.5.cloned.1.call-update) | async-done | bytes 196624 | tf_op jit(solution)/shard_map/psum | solution.py:83
  1358.9 1.6 copy.60
  (69 shorter events, 6.5 us)
Async XLA Ops:
  7.2 320.2 %copy-start = (bf16[6144,128]{1,0:T(8,128)(2,1)S(1)}, bf16[6144,128]{1,0:T(8,128)(2,1)}, u32[]{:S(2)}) copy-start(bf16[6144,128]{1,0:T(8,128)(2,1)} %param.10) | copy-start | bytes 4718596
  15.7 21.0 %copy-start.10 = (bf16[384,128]{1,0:T(8,128)(2,1)S(1)}, bf16[384,128]{1,0:T(8,128)(2,1)}, u32[]{:S(2)}) copy-start(bf16[384,128]{1,0:T(8,128)(2,1)} %param.11) | copy-start | bytes 294916
  15.7 21.8 %copy-start.6 = (bf16[8,6144]{1,0:T(8,128)(2,1)S(1)}, bf16[8,6144]{1,0:T(8,128)(2,1)}, u32[]{:S(2)}) copy-start(bf16[8,6144]{1,0:T(8,128)(2,1)} %param.6) | copy-start | bytes 294916
  15.7 21.8 %copy-start.8 = (bf16[6144,8]{0,1:T(8,128)(2,1)S(1)}, bf16[6144,8]{0,1:T(8,128)(2,1)}, u32[]{:S(2)}) copy-start(bf16[6144,8]{0,1:T(8,128)(2,1)} %param.8) | copy-start | bytes 294916
  15.7 22.0 %copy-start.13 = (s32[8,2]{0,1:T(2,128)S(1)}, s32[8,2]{0,1:T(2,128)}, u32[]{:S(2)}) copy-start(s32[8,2]{0,1:T(2,128)} %param.7) | copy-start | bytes 196
  15.7 295.3 %all-to-all-start.1 = ((bf16[128,3,6144]{2,1,0:T(4,128)(2,1)}), bf16[128,3,6144]{2,1,0:T(4,128)(2,1)}, u32[]{:S(2)}, u32[]{:S(2)}) async-start(bf16[128,3,6144]{2,1,0:T(4,128)(2,1)} %bitcast.35), calls=%async_computation.1 | async-start | bytes 12582912 | tf_op jit(solution)/shard_map/all_to_all | solution.py:47
  38.5 284.9 %copy-start.3 = (bf16[6144,128]{1,0:T(8,128)(2,1)S(1)}, bf16[6144,128]{1,0:T(8,128)(2,1)}, u32[]{:S(2)}) copy-start(bf16[6144,128]{1,0:T(8,128)(2,1)} %param.9) | copy-start | bytes 4718596
  323.4 3.9 copy-start.2
  323.4 3.9 copy-start.4
  329.7 27.2 %all-to-all-start.3 = ((f32[128,3,1]{1,2,0:T(1,128)}), f32[128,3,1]{1,2,0:T(1,128)}, u32[]{:S(2)}, u32[]{:S(2)}) async-start(f32[128,3,1]{1,2,0:T(1,128)} %bitcast.36), calls=%async_computation.3 | async-start | bytes 131072 | tf_op jit(solution)/shard_map/all_to_all | solution.py:67
  343.7 16.2 %copy-start.15 = (s32[8,2]{0,1:T(2,128)}, s32[8,2]{0,1:T(2,128)S(1)}, u32[]{:S(2)}) copy-start(s32[8,2]{0,1:T(2,128)S(1)} %copy.45) | copy-start | bytes 196
  368.8 1.2 copy-start.11
  397.3 2.4 copy-start.5
  419.2 7.0 copy-start.12
  419.2 7.0 copy-start.17
  419.2 7.1 copy-start.14
  419.2 552.0 %all-to-all-start.2 = ((f32[128,3,6144]{2,1,0:T(4,128)}), f32[128,3,6144]{2,1,0:T(4,128)}, u32[]{:S(2)}, u32[]{:S(2)}) async-start(f32[128,3,6144]{2,1,0:T(4,128)} %all_to_all.28), calls=%async_computation.2 | async-start | bytes 25165824 | tf_op jit(solution)/shard_map/all_to_all | solution.py:66
  426.2 602.1 %all-reduce.3.cloned.1.call-start = ((), (), s32[]{:S(2)}) async-start(), calls=%async_computation.4 | async-start | bytes 393216 | tf_op jit(solution)/shard_map/psum | solution.py:76
  426.3 551.8 %copy-start.16 = (s32[8,2]{0,1:T(2,128)S(1)}, s32[8,2]{0,1:T(2,128)}, u32[]{:S(2)}) copy-start(s32[8,2]{0,1:T(2,128)} %copy-done.15) | copy-start | bytes 196
  426.4 552.9 %copy-start.7 = (bf16[8,6144]{1,0:T(8,128)(2,1)S(1)}, bf16[8,6144]{1,0:T(8,128)(2,1)}, u32[]{:S(2)}) copy-start(bf16[8,6144]{1,0:T(8,128)(2,1)} %param.6) | copy-start | bytes 294916
  426.4 602.0 %copy-start.9 = (bf16[6144,8]{0,1:T(8,128)(2,1)S(1)}, bf16[6144,8]{0,1:T(8,128)(2,1)}, u32[]{:S(2)}) copy-start(bf16[6144,8]{0,1:T(8,128)(2,1)} %param.8) | copy-start | bytes 294916
  971.2 389.3 %copy-start.1 = (bf16[6144,128]{1,0:T(8,128)(2,1)S(1)}, bf16[6144,128]{1,0:T(8,128)(2,1)}, u32[]{:S(2)}) copy-start(bf16[6144,128]{1,0:T(8,128)(2,1)} %param.10) | copy-start | bytes 4718596
  979.2 379.7 %all-reduce.5.cloned.1.call-start = ((), (), s32[]{:S(2)}) async-start(), calls=%async_computation.5 | async-start | bytes 393216 | tf_op jit(solution)/shard_map/psum | solution.py:83
Sparse Core Ops, SparseCore 0:
  979.4 48.9 all-reduce.2
  1032.2 326.7 all-reduce.4
where the time goes:
time: 1370 us
  waiting for transfers between devices  1210 us (88%)
  local copies, waits for them, and re-layouts  42.8 us (3%)
  starting transfers between devices  40.7 us (3%)
  blocking collectives  31.8 us (2%)
  matrix products  19.3 us (1%)
  between operations  14.3 us (1%)
    all_to_all x1, waiting for transfers between devices, local(): lax.all_to_all(slot_dx, 'seq', split_axis=0, concat_axis=0, tiled=True)  545 us
    psum x1, waiting for transfers between devices, local(): grad_router = lax.psum(router_part, 'seq')  329 us
    all_to_all x1, waiting for transfers between devices, local(): lax.all_to_all(outgoing, 'seq', split_axis=0, concat_axis=0, tiled=True)  272 us
    psum x1, waiting for transfers between devices, local(): token_dx, pair_dp = lax.psum((token_dx, pair_dp), 'sect')  47.2 us
  transfers between devices with their start and end apart: 5, of which 5 were waited for; matrix products, arithmetic and copies ran while one was open for 0% of the time, Pallas kernels for 0%

commit v1 on v0

v1 whole, which is shorter than its diff:
```python
import jax
import jax.numpy as jnp
from jax import lax
from jax.experimental import pallas as pl
from jax.experimental.pallas import tpu as pltpu
from jax.sharding import Mesh, PartitionSpec as P

AXES = ("sect", "e", "zl", "x", "core")
bf16, f32, i32 = jnp.bfloat16, jnp.float32, jnp.int32
Y, E, Z, X, C = 4, 8, 2, 4, 2
MOST = 3
LIMIT = 48 * 1024 * 1024


def iota(shape, dim):
    return lax.broadcasted_iota(i32, shape, dim)


def split2(v):
    hi = v.astype(bf16).astype(f32)
    return hi, v - hi


def pre_kernel(rows_ref, w_ref, own_ref, part_ref):
    step = pl.program_id(0)
    rows = jnp.concatenate([rows_ref[i, 0:96, :] for i in range(X)], axis=0)
    got = jnp.dot(rows, w_ref[...], preferred_element_type=f32)
    own = jnp.concatenate([got[:, 0:256], got[:, 512:640]], axis=1)
    part = got[:, 256:640]

    @pl.when(step == 0)
    def _():
        own_ref[...] = own
        part_ref[...] = part

    @pl.when(step != 0)
    def _():
        own_ref[...] += own
        part_ref[...] += part


def act_kernel(expert_ref, own_ref, recv_ref, cot_ref, rows_ref, hidden_ref, d_ref, coef_ref):
    slots = own_ref.shape[0]
    gate = own_ref[:, 0:128] + recv_ref[:, 0:128]
    up = own_ref[:, 128:256] + recv_ref[:, 128:256]
    logits = own_ref[:, 256:384] + recv_ref[:, 256:384]
    eye = iota((96, 128), 0) == iota((96, 128), 1)
    other = jnp.concatenate(
        [
            jnp.sum(
                jnp.where(eye, rows_ref[i, 96:104, 0:128].astype(f32)[0:1, :], 0.0),
                axis=1,
                keepdims=True,
            )
            for i in range(X)
        ],
        axis=0,
    )
    lane = iota((slots, 128), 1)
    valid = other > 0.5
    mine = lane == expert_ref[0]
    its = lane == (other - 1.0).astype(i32)
    own_logit = jnp.sum(jnp.where(mine, logits, 0.0), axis=1, keepdims=True)
    other_logit = jnp.sum(jnp.where(its, logits, 0.0), axis=1, keepdims=True)
    top = jnp.maximum(own_logit, other_logit)
    a, b = jnp.exp(own_logit - top), jnp.exp(other_logit - top)
    prob = jnp.where(valid, a / (a + b), 0.0)
    both = jnp.where(valid, (a / (a + b)) * (b / (a + b)), 0.0)
    weight = prob.astype(bf16).astype(f32)
    sigma = jax.nn.sigmoid(gate)
    act = gate * sigma * up
    hidden_ref[...] = (weight * act).astype(bf16)
    grad_out = cot_ref[...].astype(f32)
    dp = jnp.sum(grad_out * act, axis=1, keepdims=True)
    d_gate = grad_out * weight * up * sigma * (1.0 + gate * (1.0 - sigma))
    d_up = grad_out * weight * gate * sigma
    hi, rest = split2(dp)
    lo, last = split2(rest)
    d_ref[:, 0:128] = d_gate.astype(bf16)
    d_ref[:, 128:256] = d_up.astype(bf16)
    d_ref[:, 256:384] = jnp.where(
        lane == 0, hi, jnp.where(lane == 1, lo, jnp.where(lane == 2, last, 0.0))
    ).astype(bf16)
    third = lane % E
    used = lane < 3 * E
    sign = jnp.where(third == expert_ref[0], 1.0, 0.0) - jnp.where(
        third == (other - 1.0).astype(i32), 1.0, 0.0
    )
    coef_ref[...] = jnp.where(used, sign * both, 0.0)


def dx_kernel(d_ref, recv_ref, coef_ref, w_ref, rows_ref, out_ref):
    slots = d_ref.shape[0]
    rows = jnp.concatenate([rows_ref[i, 0:96, :] for i in range(X)], axis=0)
    dims = (((1,), (1,)), ((), ()))
    dx = lax.dot_general(d_ref[:, 0:256], w_ref[:, 0:256], dims, preferred_element_type=f32)
    dx = dx + lax.dot_general(
        recv_ref[:, 0:256], w_ref[:, 256:512], dims, preferred_element_type=f32
    )
    dp = jnp.sum(d_ref[:, 256:384].astype(f32), axis=1, keepdims=True)
    dp_recv = jnp.sum(recv_ref[:, 256:384].astype(f32), axis=1, keepdims=True)
    coef = coef_ref[...] * (dp + dp_recv)
    hi, rest = split2(coef)
    lo, last = split2(rest)
    lane = iota((slots, 128), 1)
    three = jnp.where(lane < E, hi, jnp.where(lane < 2 * E, lo, last)).astype(bf16)
    got = lax.dot_general(three, rows, (((0,), (0,)), ((), ())), preferred_element_type=f32)
    router = got[0:E] + got[E : 2 * E] + got[2 * E : 3 * E]
    router_hi, router_lo = split2(router)
    dp_hi, dp_lo = split2(dp)
    eye = iota((96, 128), 0) == iota((96, 128), 1)
    width = dx.shape[1]
    for i in range(X):
        part = slice(i * 96, (i + 1) * 96)
        out_ref[i, 0:96, :] = dx[part].astype(bf16)
        dp_row = [
            jnp.pad(
                jnp.sum(jnp.where(eye, v[part], 0.0), axis=0, keepdims=True),
                ((0, 0), (0, width - 128)),
            )
            for v in (dp_hi, dp_lo)
        ]
        meta = jnp.concatenate(
            [
                router_hi[2 * i : 2 * i + 2],
                router_lo[2 * i : 2 * i + 2],
                *dp_row,
                jnp.zeros((2, width), f32),
            ],
            axis=0,
        )
        out_ref[i, 96:104, :] = meta.astype(bf16)


def sum_kernel(recv_ref, out_ref, acc_ref):
    step = pl.program_id(0)
    total = jnp.sum(recv_ref[...].astype(f32), axis=0)

    @pl.when(step == 0)
    def _():
        acc_ref[...] = total

    @pl.when(step != 0)
    def _():
        acc_ref[...] += total

    @pl.when(step == pl.num_programs(0) - 1)
    def _():
        main = acc_ref[0:96, :]
        meta = acc_ref[96:104, :]
        router_hi, router_lo = split2(meta[0:2] + meta[2:4])
        dp_hi, dp_lo = split2(meta[4:5, 0:128] + meta[5:6, 0:128])
        dp_row = jnp.concatenate([jnp.zeros((1, 512), f32), dp_hi, dp_lo], axis=1)
        source = jnp.concatenate(
            [main, router_hi, router_lo, dp_row, jnp.zeros((3, 768), f32)], axis=0
        ).astype(bf16)
        row = iota((256, 104), 0)
        column = iota((256, 104), 1)
        place, q = row // 8, row % 8
        core = place % 2

        def pick(cases):
            target = jnp.full((256, 104), -1, i32)
            for value, where in cases:
                target = jnp.where(q == value, where, target)
            return jnp.where(column == target, 1.0, 0.0).astype(bf16)

        hi, lo, dp = 96 + core, 98 + core, 100
        first = pick(
            [(0, 3 * place), (1, 3 * place + 1), (2, 3 * place + 2), (5, hi), (6, lo)]
        )
        left = pick([(3, 3 * place), (4, 3 * place + 2), (7, lo)])
        right = pick([(3, 3 * place + 1), (4, hi), (7, jnp.full((256, 104), dp, i32))])
        got = jnp.dot(first, source[:, 0:512], preferred_element_type=f32)
        tail = source[:, 512:768]
        out_ref[:, 0:256] = (
            got[:, 0:256] + jnp.dot(left, tail, preferred_element_type=f32)
        ).astype(bf16)
        out_ref[:, 256:512] = (
            got[:, 256:512] + jnp.dot(right, tail, preferred_element_type=f32)
        ).astype(bf16)


def call(kernel, grid, in_specs, out_specs, out_shape, scratch=()):
    return pl.pallas_call(
        kernel,
        grid=grid,
        in_specs=in_specs,
        out_specs=out_specs,
        out_shape=out_shape,
        scratch_shapes=list(scratch),
        compiler_params=pltpu.CompilerParams(vmem_limit_bytes=LIMIT),
    )


def whole(*shape):
    return pl.BlockSpec(shape, lambda *_: (0,) * len(shape))


def a2a(v, axes):
    return lax.all_to_all(v, axes, split_axis=0, concat_axis=0, tiled=True)


def everywhere(v, count):
    return jnp.broadcast_to(v[None], (count,) + v.shape)


def swap(v):
    return lax.ppermute(v, "core", [(0, 1), (1, 0)])


def local(tokens, routes, w_router, w_gate, w_up, cotangent):
    tok, width = tokens.shape
    half, piece = width // C, width // (C * Y)
    core, sect, expert = lax.axis_index("core"), lax.axis_index("sect"), lax.axis_index("e")
    slots = cotangent.shape[0]
    sds = jax.ShapeDtypeStruct

    pairs = routes.reshape(-1)
    count = tok * 2
    same = pairs[:, None] == pairs[None, :]
    earlier = jnp.arange(count)[None, :] < jnp.arange(count)[:, None]
    ranks = jnp.sum((same & earlier).astype(i32), axis=1)
    places = pairs * MOST + ranks
    select = (places[None, :] == jnp.arange(E * MOST, dtype=i32)[:, None]).astype(f32)
    others = routes[:, ::-1].reshape(-1).astype(f32) + 1.0
    other_of = jnp.sum(select * others[None, :], axis=1)
    by_token = jnp.sum(select.reshape(E * MOST, tok, 2), axis=2).astype(bf16)

    mine = lax.dynamic_index_in_dim(
        tokens.reshape(tok, C, Y, piece), sect, axis=2, keepdims=False
    ).reshape(tok, C * piece)
    picked = jnp.dot(by_token, mine, preferred_element_type=f32).astype(bf16)
    picked = picked.reshape(E, MOST, C, piece).transpose(0, 2, 1, 3)
    note = jnp.pad(other_of.reshape(E, 1, 1, MOST), ((0, 0), (0, 0), (0, 0), (0, piece - MOST)))
    note = jnp.broadcast_to(note, (E, C, 1, piece)).astype(bf16)
    out = jnp.concatenate([picked, note], axis=2)
    out = jnp.broadcast_to(out[:, None], (E, Z, C, MOST + 1, piece))
    arrived = a2a(out.reshape(E * Z * C, MOST + 1, piece), ("e", "zl", "core"))

    block = arrived[:, 0:MOST, :].reshape(E * Z * C * MOST, piece)
    notes = arrived[:, MOST, 0:MOST].reshape(1, E * Z * C * MOST)
    notes = jnp.pad(notes, ((0, 7), (0, piece - E * Z * C * MOST)))
    block = jnp.concatenate([block, notes], axis=0)
    rows = a2a(everywhere(block, Y * X), ("sect", "x"))

    both = jnp.concatenate([w_gate, w_up], axis=1)
    own_w = lax.dynamic_slice_in_dim(both, core * half, half, 0)
    sent_w = lax.dynamic_slice_in_dim(both, (1 - core) * half, half, 0)
    router_half = lax.dynamic_slice_in_dim(w_router, core * half, half, 0)
    weights = jnp.concatenate(
        [own_w, swap(sent_w), jnp.pad(router_half, ((0, 0), (0, 128 - E)))], axis=1
    )
    cot = cotangent.reshape(E * Z, X, C * MOST, 128).transpose(1, 0, 2, 3).reshape(slots, 128)

    rows_spec = pl.BlockSpec((X, 104, piece), lambda i: (i, 0, 0))
    w_spec = pl.BlockSpec((piece, 640), lambda i: (i, 0))
    own, part = call(
        pre_kernel,
        (Y,),
        [rows_spec, w_spec],
        [whole(slots, 384), whole(slots, 384)],
        [sds((slots, 384), f32), sds((slots, 384), f32)],
    )(rows, weights)
    hidden, d, coef = call(
        act_kernel,
        (1,),
        [
            pl.BlockSpec(memory_space=pltpu.SMEM),
            whole(slots, 384),
            whole(slots, 384),
            whole(slots, 128),
            whole(X, 104, piece),
        ],
        [whole(slots, 128), whole(slots, 384), whole(slots, 128)],
        [sds((slots, 128), bf16), sds((slots, 384), bf16), sds((slots, 128), f32)],
    )(expert.reshape(1).astype(i32), own, swap(part), cot, rows)
    hidden = hidden.reshape(X, E * Z, C * MOST, 128).transpose(1, 0, 2, 3).reshape(slots, 128)

    back = call(
        dx_kernel,
        (Y,),
        [whole(slots, 384), whole(slots, 384), whole(slots, 128), w_spec, rows_spec],
        rows_spec,
        sds((Y * X, 104, piece), bf16),
    )(d, swap(d), coef, weights, rows)

    back = a2a(back, ("sect", "x"))
    summed = call(
        sum_kernel,
        (Y,),
        [rows_spec],
        whole(256, 512),
        sds((256, 512), bf16),
        [pltpu.VMEM((104, piece), f32)],
    )(back)
    home = a2a(summed.reshape(E * Z * C, 8, 512), ("e", "zl", "core"))
    home = home.reshape(E, Z, C, 8, 512)

    tails = [home[:, :, :, 3, 0:256], home[:, :, :, 3, 256:512], home[:, :, :, 4, 0:256]]
    main = jnp.concatenate([home[:, :, :, 0:3, :], jnp.stack(tails, axis=3)], axis=4)
    spread = by_token.T.reshape(tok, E, MOST)
    token_dx = jnp.einsum("ter,ezcrd->tcd", spread, main, preferred_element_type=f32)
    router_parts = jnp.concatenate(
        [
            home[:, :, :, 5, :].astype(f32) + home[:, :, :, 6, :].astype(f32),
            home[:, :, :, 4, 256:512].astype(f32) + home[:, :, :, 7, 0:256].astype(f32),
        ],
        axis=3,
    )
    router = jnp.sum(router_parts, axis=(0, 1))
    dp = jnp.sum(home[:, :, :, 7, 256:512].astype(f32), axis=(1, 2))
    dp = dp[:, 0:128] + dp[:, 128:256]
    place = (expert * Z + lax.axis_index("zl")) * C + core
    dp = lax.dynamic_slice_in_dim(dp, place * MOST, MOST, 1).reshape(E * MOST)
    pair_dp = jnp.sum(select * dp[:, None], axis=0).reshape(tok, 2)

    logits = jnp.dot(tokens, w_router, preferred_element_type=f32)
    choose = (routes[:, :, None] == jnp.arange(E, dtype=i32)[None, None, :]).astype(f32)
    probs = jax.nn.softmax(jnp.sum(choose * logits[:, None, :], axis=2), axis=1)
    mean_dp = jnp.sum(probs * pair_dp, axis=1, keepdims=True)
    d_pick = probs * (pair_dp - mean_dp)
    d_logits = jnp.sum(choose * d_pick[:, :, None], axis=1)
    w_mine = lax.dynamic_index_in_dim(
        w_router.reshape(C, Y, piece, E), sect, axis=1, keepdims=False
    ).astype(f32)
    router_dx = jnp.einsum("te,cde->tcd", d_logits, w_mine, precision=lax.Precision.HIGHEST)
    grad_tokens = (token_dx + router_dx).astype(bf16).reshape(tok, C * piece)

    router = router.reshape(1, C * piece)
    hi = lax.reduce_precision(router, 8, 7)
    lo = router - hi
    pack = jnp.concatenate([grad_tokens, hi.astype(bf16), lo.astype(bf16)], axis=0)
    got = a2a(everywhere(pack, Y), ("sect",))
    grad_tokens = got[:, 0:tok, :].reshape(Y, tok, C, piece).transpose(1, 2, 0, 3)
    mine_router = got[:, tok, :].astype(f32) + got[:, tok + 1, :].astype(f32)
    mine_router = mine_router.reshape(Y, C, piece).transpose(1, 0, 2).reshape(8, width // 8)
    grad_router = a2a(everywhere(mine_router, X * C), ("x", "core"))
    return hidden, grad_tokens.reshape(tok, width), grad_router.reshape(E, width).T


def solution(mesh):
    fine = Mesh(mesh.devices.reshape(Y, E, Z, X, C), AXES)
    seq = ("e", "zl", "x", "core")
    columns = P(None, seq + ("sect",))
    return jax.shard_map(
        local,
        mesh=fine,
        in_specs=(P(seq, None), P(seq, None), P(), columns, columns, columns),
        out_specs=(columns, P(seq, None), P()),
        check_vma=False,
    )
```

time: 1370 us -> 199 us (0.15)
  waiting for transfers between devices: 1210 us -> 65.4 us
  local copies, waits for them, and re-layouts: 42.8 us -> 19.2 us
  matrix products: 19.3 us -> 0.8 us
    all_to_all x3 -> x4, waiting for transfers between devices: 831 us -> 61 us  [a2a(): return lax.all_to_all(v, axes, split_axis=0, concat_axis=0, tiled=True)]
    psum x2 -> x0, waiting for transfers between devices: 376 us -> none  [the longest x1 329 us: local(): grad_router = lax.psum(router_part, 'seq')]
    all_to_all x3 -> x0, local copies, waits for them, and re-layouts: 27.7 us -> none  [the longest x1 14.5 us: local(): lax.all_to_all(slot_dx, 'seq', split_axis=0, concat_axis=0, tiled=True)]
    all_to_all x1 -> x2, blocking collectives: 23 us -> 42.8 us  [a2a(): return lax.all_to_all(v, axes, split_axis=0, concat_axis=0, tiled=True)]
    dot_general x11 -> x4, matrix products: 19.3 us -> 0.8 us  [the longest x1 0.28 us: local(): jnp.einsum('ter,ezcrd->tcd', spread, main, preferred_element_type=f32)]
    all_to_all x3 -> x4, starting transfers between devices: 40.6 us -> 38.5 us  [a2a(): return lax.all_to_all(v, axes, split_axis=0, concat_axis=0, tiled=True)]
  transfers between devices with their start and end apart: 5 -> 7, of which waited for: 5 -> 7; matrix products, arithmetic and copies ran while one was open for 0% -> 7% of each run, Pallas kernels for 0% -> 0%
where the time goes in v1:
time: 199 us; the launch traced here: 198 us
  waiting for transfers between devices  65.4 us (33%)
  starting transfers between devices  49.6 us (25%)
  blocking collectives  42.8 us (22%)
  local copies, waits for them, and re-layouts  19.2 us (10%)
  Pallas kernels  13.1 us (7%)
  other arithmetic  5.95 us (3%)
    all_to_all x4, waiting for transfers between devices, a2a(): return lax.all_to_all(v, axes, split_axis=0, concat_axis=0, tiled=True)  61 us
    all_to_all x2, blocking collectives, a2a(): return lax.all_to_all(v, axes, split_axis=0, concat_axis=0, tiled=True)  42.8 us
    all_to_all x4, starting transfers between devices, a2a(): return lax.all_to_all(v, axes, split_axis=0, concat_axis=0, tiled=True)  38.5 us
    ppermute x3, starting transfers between devices, swap(): return lax.ppermute(v, 'core', [(0, 1), (1, 0)])  11.1 us
    pallas_call x1, Pallas kernels, local(): call(pre_kernel, (Y,), [rows_spec, w_spec], [whole(slots, 384), whole(slo...  5.49 us
    ppermute x3, waiting for transfers between devices, swap(): return lax.ppermute(v, 'core', [(0, 1), (1, 0)])  4.4 us
    pallas_call x1, Pallas kernels, local(): call(dx_kernel, (Y,), [whole(slots, 384), whole(slots, 384), whole(slots,...  4.37 us
  transfers between devices with their start and end apart: 7, of which 7 were waited for; matrix products, arithmetic and copies ran while one was open for 7% of the time, Pallas kernels for 0%

profile of v1, /device:TPU:1, one launch (start us, length us, event | category | flops | bytes accessed | tf_op | source)
XLA Modules:
  0.0 198.0 jit_solution(17964409962698037573)
XLA Ops:
  0.6 0.8 copy.57
  1.8 0.7 rev.3
  2.7 0.7 constant_dynamic-slice_fusion.4
  4.2 0.7 broadcast_in_dim.13
  5.0 16.7 %all-to-all-start = ((bf16[32,4,768]{2,1,0:T(4,128)(2,1)}), bf16[32,4,768]{2,1,0:T(4,128)(2,1)S(1)}, u32[]{:S(2)}, u32[]{:S(2)}) async-start(bf16[32,4,768]{2,1,0:T(4,128)(2,1)} %bitcast.5), calls=%async_computation | async-start | bytes 393216 | tf_op jit(solution)/shard_map/all_to_all | solution.py:201
  21.7 1.7 constant_dynamic-update-slice_fusion.1
  23.4 1.8 constant_dynamic-update-slice_fusion
  25.2 15.1 %all-to-all-done = bf16[32,4,768]{2,1,0:T(4,128)(2,1)S(1)} async-done(((bf16[32,4,768]{2,1,0:T(4,128)(2,1)}), bf16[32,4,768]{2,1,0:T(4,128)(2,1)S(1)}, u32[]{:S(2)}, u32[]{:S(2)}) %all-to-all-start) | async-done | bytes 196640 | tf_op jit(solution)/shard_map/all_to_all | solution.py:201
  40.3 0.8 reshape.229
  41.3 0.9 fusion.4
  42.2 1.6 broadcast_in_dim.14
  43.9 6.8 %all-to-all-start.1 = ((bf16[16,104,768]{2,1,0:T(8,128)(2,1)}), bf16[16,104,768]{2,1,0:T(8,128)(2,1)S(1)}, u32[]{:S(2)}, u32[]{:S(2)}) async-start(bf16[16,104,768]{2,1,0:T(8,128)(2,1)} %broadcast_in_dim.14), calls=%async_computation.1 | async-start | bytes 5111808 | tf_op jit(solution)/shard_map/all_to_all | solution.py:201
  50.6 3.8 %constant_dynamic-slice_fusion.3 = (bf16[3072,256]{1,0:T(8,128)(2,1)}, bf16[3072,256]{1,0:T(8,128)(2,1)}) fusion(bf16[6144,256]{1,0:T(8,128)(2,1)} %copy-done.1, s32[]{:T(128)S(6)} %select_n.17, s32[]{:T(128)S(6)} %select_n.18), kind=kLoop, calls=%fused_computation.57 | loop fusion | bytes 6291464 | tf_op jit(solution)/shard_map/dynamic_slice | solution.py:248
  54.4 3.8 %collective-permute-start = (bf16[3072,256]{1,0:T(8,128)(2,1)}, bf16[3072,256]{1,0:T(8,128)(2,1)}, u32[]{:S(2)}, u32[]{:S(2)}) collective-permute-start(bf16[3072,256]{1,0:T(8,128)(2,1)} %get-tuple-element.16), channel_id=1, source_target_pairs={{0,1},{1,0},{2,3},{3,2},{4,5},{5,4},{6,7},{7,6},{8,9},{9,8},{10,11... | collective-permute-start | bytes 4718600 | tf_op jit(solution)/shard_map/ppermute | solution.py:209
  58.7 2.9 %collective-permute-done = bf16[3072,256]{1,0:T(8,128)(2,1)} collective-permute-done((bf16[3072,256]{1,0:T(8,128)(2,1)}, bf16[3072,256]{1,0:T(8,128)(2,1)}, u32[]{:S(2)}, u32[]{:S(2)}) %collective-permute-start) | collective-permute-done | bytes 1572896 | tf_op jit(solution)/shard_map/ppermute | solution.py:209
  61.6 3.4 %fusion.1.w_ref = bf16[3072,640]{1,0:T(8,128)(2,1)} fusion(bf16[3072,8]{1,0:T(8,128)(2,1)S(1)} %copy.78, bf16[3072,256]{1,0:T(8,128)(2,1)} %collective-permute-done, bf16[3072,256]{1,0:T(8,128)(2,1)} %get-tuple-element.15), kind=kLoop, calls=%fused_computation.2 | loop fusion | flops 15728640 | bytes 7127040 | tf_op jit(solution)/shard_map/concatenate | solution.py:251
  65.0 20.2 %all-to-all-done.1.rows_ref = bf16[16,104,768]{2,1,0:T(8,128)(2,1)S(1)} async-done(((bf16[16,104,768]{2,1,0:T(8,128)(2,1)}), bf16[16,104,768]{2,1,0:T(8,128)(2,1)S(1)}, u32[]{:S(2)}, u32[]{:S(2)}) %all-to-all-start.1) | async-done | bytes 2555936 | tf_op jit(solution)/shard_map/all_to_all | solution.py:201
  85.2 5.5 %shard_map.85 = (f32[384,384]{1,0:T(8,128)S(1)}, f32[384,384]{1,0:T(8,128)}) custom-call(bf16[16,104,768]{2,1,0:T(8,128)(2,1)S(1)} %all-to-all-done.1.rows_ref, bf16[3072,640]{1,0:T(8,128)(2,1)} %fusion.1.w_ref), custom_call_target="tpu_custom_call" | custom-call | tf_op jit(solution)/shard_map/pallas_call | solution.py:258
  90.7 5.0 %collective-permute-start.1 = (f32[384,384]{1,0:T(8,128)}, f32[384,384]{1,0:T(8,128)}, u32[]{:S(2)}, u32[]{:S(2)}) collective-permute-start(f32[384,384]{1,0:T(8,128)} %get-tuple-element.9), channel_id=1, source_target_pairs={{0,1},{1,0},{2,3},{3,2},{4,5},{5,4},{6,7},{7,6},{8,9},{9,8},{10,11... | collective-permute-start | bytes 1769480 | tf_op jit(solution)/shard_map/ppermute | solution.py:209
  96.4 0.9 reshape.231.cot_ref
  97.6 1.7 shard_map.86
  99.3 2.3 %collective-permute-start.2 = (bf16[384,384]{1,0:T(8,128)(2,1)S(1)}, bf16[384,384]{1,0:T(8,128)(2,1)S(1)}, u32[]{:S(2)}, u32[]{:S(2)}) collective-permute-start(bf16[384,384]{1,0:T(8,128)(2,1)S(1)} %get-tuple-element.11.d_ref), channel_id=1, source_target_pairs={{0,1},{1,0},{2,3},{3,2},{4,5},{5,4},{6,7},{7,6},{8,9},{9,8},{10,11... | collective-permute-start | bytes 884744 | tf_op jit(solution)/shard_map/ppermute | solution.py:209
  101.6 1.2 collective-permute-done.2.recv_ref
  102.8 4.4 %shard_map.87 = bf16[16,104,768]{2,1,0:T(8,128)(2,1)S(1)} custom-call(bf16[384,384]{1,0:T(8,128)(2,1)S(1)} %get-tuple-element.11.d_ref, bf16[384,384]{1,0:T(8,128)(2,1)S(1)} %collective-permute-done.2.recv_ref, f32[384,128]{1,0:T(8,128)S(1)} %get-tuple-element.12.coef_ref, bf16[3072,640]{1,0:T(8,128)(2,1)} %fusion.1.w_ref, ...), custom_call_target="tpu_custom_call" | custom-call | tf_op jit(solution)/shard_map/pallas_call | solution.py:280
  107.2 35.3 %all_to_all.30.recv_ref = bf16[16,104,768]{2,1,0:T(8,128)(2,1)S(1)} all-to-all(bf16[16,104,768]{2,1,0:T(8,128)(2,1)S(1)} %shard_map.87), channel_id=1, replica_groups=mesh['sect'=4,'e'=8,'zl'=2,'x'=4,'core'=2] {'sect','x'}, dimensions={0} | all-to-all | bytes 5111808 | tf_op jit(solution)/shard_map/all_to_all | solution.py:201
  142.5 1.6 shard_map.88
  144.1 9.5 %all-to-all-start.3 = ((bf16[32,8,512]{2,1,0:T(8,128)(2,1)}), bf16[32,8,512]{2,1,0:T(8,128)(2,1)S(1)}, u32[]{:S(2)}, u32[]{:S(2)}) async-start(bf16[32,8,512]{2,1,0:T(8,128)(2,1)} %bitcast.10), calls=%async_computation.3 | async-start | bytes 524288 | tf_op jit(solution)/shard_map/all_to_all | solution.py:201
  154.3 21.4 %all-to-all-done.3 = bf16[32,8,512]{2,1,0:T(8,128)(2,1)S(1)} async-done(((bf16[32,8,512]{2,1,0:T(8,128)(2,1)}), bf16[32,8,512]{2,1,0:T(8,128)(2,1)S(1)}, u32[]{:S(2)}, u32[]{:S(2)}) %all-to-all-start.3) | async-done | bytes 262176 | tf_op jit(solution)/shard_map/all_to_all | solution.py:201
  177.5 7.5 %all_to_all.31 = bf16[4,10,1536]{2,1,0:T(8,128)(2,1)S(1)} all-to-all(bf16[4,10,1536]{2,1,0:T(8,128)(2,1)S(1)} %broadcast_in_dim.15), channel_id=1, replica_groups=mesh['sect'=4,'e'=8,'zl'=2,'x'=4,'core'=2] {'sect'}, dimensions={0} | all-to-all | bytes 245760 | tf_op jit(solution)/shard_map/all_to_all | solution.py:201
  185.9 5.4 %all-to-all-start.5 = ((f32[8,8,768]{2,1,0:T(8,128)}), f32[8,8,768]{2,1,0:T(8,128)S(1)}, u32[]{:S(2)}, u32[]{:S(2)}) async-start(f32[8,8,768]{2,1,0:T(8,128)} %broadcast_in_dim.17), calls=%async_computation.5 | async-start | bytes 393216 | tf_op jit(solution)/shard_map/all_to_all | solution.py:201
  192.9 4.4 %all-to-all-done.5 = f32[8,8,768]{2,1,0:T(8,128)S(1)} async-done(((f32[8,8,768]{2,1,0:T(8,128)}), f32[8,8,768]{2,1,0:T(8,128)S(1)}, u32[]{:S(2)}, u32[]{:S(2)}) %all-to-all-start.5) | async-done | bytes 196640 | tf_op jit(solution)/shard_map/all_to_all | solution.py:201
  197.3 0.7 copy.81
  (76 shorter events, 7.6 us)
Async XLA Ops:
  0.6 57.6 %copy-start = (bf16[6144,8]{0,1:T(8,128)(2,1)S(1)}, bf16[6144,8]{0,1:T(8,128)(2,1)}, u32[]{:S(2)}) copy-start(bf16[6144,8]{0,1:T(8,128)(2,1)} %param.8) | copy-start | bytes 294916
  5.0 35.4 %all-to-all-start = ((bf16[32,4,768]{2,1,0:T(4,128)(2,1)}), bf16[32,4,768]{2,1,0:T(4,128)(2,1)S(1)}, u32[]{:S(2)}, u32[]{:S(2)}) async-start(bf16[32,4,768]{2,1,0:T(4,128)(2,1)} %bitcast.5), calls=%async_computation | async-start | bytes 393216 | tf_op jit(solution)/shard_map/all_to_all | solution.py:201
  25.2 18.7 %copy-start.1 = (bf16[6144,256]{1,0:T(8,128)(2,1)}, bf16[6144,256]{1,0:T(8,128)(2,1)S(1)}, u32[]{:S(2)}) copy-start(bf16[6144,256]{1,0:T(8,128)(2,1)S(1)} %constant_dynamic-update-slice_fusion) | copy-start | bytes 9437188
  43.9 41.3 %all-to-all-start.1 = ((bf16[16,104,768]{2,1,0:T(8,128)(2,1)}), bf16[16,104,768]{2,1,0:T(8,128)(2,1)S(1)}, u32[]{:S(2)}, u32[]{:S(2)}) async-start(bf16[16,104,768]{2,1,0:T(8,128)(2,1)} %broadcast_in_dim.14), calls=%async_computation.1 | async-start | bytes 5111808 | tf_op jit(solution)/shard_map/all_to_all | solution.py:201
  54.4 7.2 %collective-permute-start = (bf16[3072,256]{1,0:T(8,128)(2,1)}, bf16[3072,256]{1,0:T(8,128)(2,1)}, u32[]{:S(2)}, u32[]{:S(2)}) collective-permute-start(bf16[3072,256]{1,0:T(8,128)(2,1)} %get-tuple-element.16), channel_id=1, source_target_pairs={{0,1},{1,0},{2,3},{3,2},{4,5},{5,4},{6,7},{7,6},{8,9},{9,8},{10,11... | collective-permute-start | bytes 4718600 | tf_op jit(solution)/shard_map/ppermute | solution.py:209
  65.0 30.7 %copy-start.3 = (bf16[384,128]{1,0:T(8,128)(2,1)S(1)}, bf16[384,128]{1,0:T(8,128)(2,1)}, u32[]{:S(2)}) copy-start(bf16[384,128]{1,0:T(8,128)(2,1)} %param.11) | copy-start | bytes 294916
  90.7 7.0 %collective-permute-start.1 = (f32[384,384]{1,0:T(8,128)}, f32[384,384]{1,0:T(8,128)}, u32[]{:S(2)}, u32[]{:S(2)}) collective-permute-start(f32[384,384]{1,0:T(8,128)} %get-tuple-element.9), channel_id=1, source_target_pairs={{0,1},{1,0},{2,3},{3,2},{4,5},{5,4},{6,7},{7,6},{8,9},{9,8},{10,11... | collective-permute-start | bytes 1769480 | tf_op jit(solution)/shard_map/ppermute | solution.py:209
  99.3 3.5 %collective-permute-start.2 = (bf16[384,384]{1,0:T(8,128)(2,1)S(1)}, bf16[384,384]{1,0:T(8,128)(2,1)S(1)}, u32[]{:S(2)}, u32[]{:S(2)}) collective-permute-start(bf16[384,384]{1,0:T(8,128)(2,1)S(1)} %get-tuple-element.11.d_ref), channel_id=1, source_target_pairs={{0,1},{1,0},{2,3},{3,2},{4,5},{5,4},{6,7},{7,6},{8,9},{9,8},{10,11... | collective-permute-start | bytes 884744 | tf_op jit(solution)/shard_map/ppermute | solution.py:209
  107.2 46.7 %copy-start.2 = (bf16[8,6144]{1,0:T(8,128)(2,1)S(1)}, bf16[8,6144]{1,0:T(8,128)(2,1)}, u32[]{:S(2)}) copy-start(bf16[8,6144]{1,0:T(8,128)(2,1)} %param.6) | copy-start | bytes 294916
  107.2 46.8 %copy-start.4 = (s32[8,2]{0,1:T(2,128)S(1)}, s32[8,2]{0,1:T(2,128)}, u32[]{:S(2)}) copy-start(s32[8,2]{0,1:T(2,128)} %param.7) | copy-start | bytes 196
  144.1 31.5 %all-to-all-start.3 = ((bf16[32,8,512]{2,1,0:T(8,128)(2,1)}), bf16[32,8,512]{2,1,0:T(8,128)(2,1)S(1)}, u32[]{:S(2)}, u32[]{:S(2)}) async-start(bf16[32,8,512]{2,1,0:T(8,128)(2,1)} %bitcast.10), calls=%async_computation.3 | async-start | bytes 524288 | tf_op jit(solution)/shard_map/all_to_all | solution.py:201
  185.9 11.3 %all-to-all-start.5 = ((f32[8,8,768]{2,1,0:T(8,128)}), f32[8,8,768]{2,1,0:T(8,128)S(1)}, u32[]{:S(2)}, u32[]{:S(2)}) async-start(f32[8,8,768]{2,1,0:T(8,128)} %broadcast_in_dim.17), calls=%async_computation.5 | async-start | bytes 393216 | tf_op jit(solution)/shard_map/all_to_all | solution.py:201

commit v2 on v0

v2 whole, which is shorter than its diff:
```python
import jax
import jax.numpy as jnp
from jax import lax
from jax.experimental import pallas as pl
from jax.experimental.pallas import tpu as pltpu
from jax.sharding import Mesh, PartitionSpec as P

AXES = ("sect", "e", "zl", "xh", "xl", "core")
HBM = pltpu.MemorySpace.HBM
bf16, f32, i32 = jnp.bfloat16, jnp.float32, jnp.int32
Y, E, Z, X, C = 4, 8, 2, 2, 2
M = Z * X
MOST = 3
GROUP = E * C * MOST
BLOCK = GROUP + 8
LIMIT = 48 * 1024 * 1024
MOST_VMEM = 60 * 1024 * 1024
LONG = pl.CostEstimate(flops=40_000_000_000, bytes_accessed=100_000_000, transcendentals=0)
LESS = pl.CostEstimate(flops=22_000_000_000, bytes_accessed=10_000_000, transcendentals=0)


def iota(shape, dim):
    return lax.broadcasted_iota(i32, shape, dim)


def split2(v):
    hi = v.astype(bf16).astype(f32)
    return hi, v - hi


def route_kernel(place_ref, routes_ref, tokens_ref, router_ref, out_ref, logits_ref):
    tok = tokens_ref.shape[0]
    piece = out_ref.shape[-1]
    sect = place_ref[0]
    logits = lax.dot_general(
        tokens_ref[...], router_ref[...], (((1,), (1,)), ((), ())), preferred_element_type=f32
    )
    logits_ref[...] = logits
    row, lane = iota((tok, E), 0), iota((tok, E), 1)
    chosen = []
    for k in range(2):
        named = jnp.zeros((tok, E), i32)
        for t in range(tok):
            named = jnp.where(row == t, routes_ref[k, t], named)
        chosen.append(jnp.sum(jnp.where(lane == named, logits, 0.0), axis=1, keepdims=True))
    top = jnp.maximum(chosen[0], chosen[1])
    a, b = jnp.exp(chosen[0] - top), jnp.exp(chosen[1] - top)
    probs = [a / (a + b), b / (a + b)]
    hi, lo = split2(probs[0] * probs[1])

    pairs = [(t, k, routes_ref[k, t], routes_ref[1 - k, t]) for t in range(tok) for k in range(2)]
    ranks = []
    for i, pair in enumerate(pairs):
        rank = jnp.int32(0)
        for j in range(i):
            rank = rank + (pairs[j][2] == pair[2]).astype(i32)
        ranks.append(rank)

    rows8, lanes8 = iota((E, 128), 0), iota((E, 128), 1)
    meta = jnp.zeros((E, 128), f32)
    for (t, k, expert, other), rank in zip(pairs, ranks):
        here = rows8 == expert
        meta = jnp.where(here & (lanes8 == rank), (other + 1).astype(f32), meta)
        for q, value in ((1, probs[k]), (2, hi), (3, lo)):
            meta = jnp.where(here & (lanes8 == q * MOST + rank), value[t : t + 1, :], meta)
    meta = jnp.concatenate([meta, jnp.zeros((E, piece - 128), f32)], axis=1)

    rows_e = iota((E, piece), 0)
    for c in range(C):
        start = pl.multiple_of((c * Y + sect) * piece, 128)
        mine = tokens_ref[:, pl.ds(start, piece)].astype(f32)
        acc = [jnp.zeros((E, piece), f32) for _ in range(MOST)]
        for (t, _, expert, _), rank in zip(pairs, ranks):
            value = jnp.broadcast_to(mine[t : t + 1, :], (E, piece))
            for r in range(MOST):
                there = rows_e == jnp.where(rank == r, expert, -1)
                acc[r] = jnp.where(there, value, acc[r])
        for e in range(E):
            rows = [v[e : e + 1] for v in (*acc, meta)]
            out_ref[e, c] = jnp.concatenate(rows, axis=0).astype(bf16)


def gather_kernel(arrived_ref, out_ref, block_ref):
    @pl.when(pl.program_id(0) == 0)
    def _():
        count = E * C
        flat = jnp.concatenate([arrived_ref[j].astype(f32) for j in range(count)], axis=0)
        flat = flat.astype(bf16)
        slot, source = iota((GROUP, 4 * count), 0), iota((GROUP, 4 * count), 1)
        pick = jnp.where(source == slot // MOST * 4 + slot % MOST, 1.0, 0.0).astype(bf16)
        block_ref[0:GROUP, :] = jnp.dot(pick, flat, preferred_element_type=f32).astype(bf16)
        pick = jnp.where(source == slot // MOST * 4 + MOST, 1.0, 0.0).astype(bf16)
        notes = jnp.dot(pick, flat[:, 0:128], preferred_element_type=f32)
        slot, lane = iota((GROUP, 128), 0), iota((GROUP, 128), 1)
        rows = []
        for q in range(4):
            column = jnp.sum(
                jnp.where(lane == q * MOST + slot % MOST, notes, 0.0), axis=1, keepdims=True
            )
            rows.append(jnp.sum(jnp.where(lane == slot, column, 0.0), axis=0, keepdims=True))
        rows.append(jnp.zeros((4, 128), f32))
        rest = jnp.zeros((8, block_ref.shape[1] - 128), f32)
        notes = jnp.concatenate([jnp.concatenate(rows, axis=0), rest], axis=1)
        block_ref[GROUP:BLOCK, :] = notes.astype(bf16)

    for i in range(M):
        out_ref[i] = block_ref[...]


def gathered_rows(rows_ref):
    return jnp.concatenate([rows_ref[i, 0:GROUP, :] for i in range(M)], axis=0)


def side(refs):
    own, near, gate, up = refs[0:4], refs[4], refs[5], refs[6]
    parts = [v[...] for v in own] + [near[0], near[1], gate[0], up[0]]
    return [jnp.concatenate(parts[i : i + 2], axis=1) for i in range(0, 8, 2)]


def half_kernel(place_ref, *refs):
    for i, ref in enumerate(refs[:-1]):
        refs[-1][i] = ref[...]


def pre_kernel(place_ref, rows_ref, *refs):
    weights, (own_ref, core_ref, flat_ref) = side(refs[0:7]), refs[7:10]
    width = rows_ref.shape[2]
    for y in range(Y):
        for i in range(M):
            flat_ref[i * GROUP : (i + 1) * GROUP, y * width : (y + 1) * width] = rows_ref[
                y * M + i, 0:GROUP, :
            ]
    for out, start, part in zip(
        (own_ref, own_ref, core_ref, core_ref), (0, 256, 0, 256), weights
    ):
        out[:, start : start + 256] = jnp.dot(flat_ref[...], part, preferred_element_type=f32)


def act_kernel(
    expert_ref, own_ref, core_ref, cot_ref, far_cot_ref, rows_ref, hidden_ref, far_ref, d_ref, coef_ref
):
    slots = own_ref.shape[0]
    eye = iota((GROUP, 128), 0) == iota((GROUP, 128), 1)

    def column(q):
        parts = []
        for i in range(M):
            notes = rows_ref[i, GROUP:BLOCK, 0:128].astype(f32)
            parts.append(jnp.sum(jnp.where(eye, notes[q : q + 1], 0.0), axis=1, keepdims=True))
        return jnp.concatenate(parts, axis=0)

    other = (column(0) - 1.0).astype(i32)
    weight = column(1)
    both = column(2) + column(3)
    dp = jnp.zeros((slots, 1), f32)
    for i, (cot, out) in enumerate(((cot_ref, hidden_ref), (far_cot_ref, far_ref))):
        first = slice(i * 256, i * 256 + 128)
        second = slice(i * 256 + 128, i * 256 + 256)
        gate = own_ref[:, first] + core_ref[:, first]
        up = own_ref[:, second] + core_ref[:, second]
        sigma = jax.nn.sigmoid(gate)
        act = gate * sigma * up
        out[...] = (weight * act).astype(bf16)
        grad_out = cot[...].astype(f32)
        dp = dp + jnp.sum(grad_out * act, axis=1, keepdims=True)
        d_gate = grad_out * weight * up * sigma * (1.0 + gate * (1.0 - sigma))
        d_up = grad_out * weight * gate * sigma
        d_ref[:, first] = d_gate.astype(bf16)
        d_ref[:, second] = d_up.astype(bf16)
    hi, rest = split2(dp)
    lo, last = split2(rest)
    lane = iota((slots, 128), 1)
    d_ref[:, 512:640] = jnp.where(
        lane == 0, hi, jnp.where(lane == 1, lo, jnp.where(lane == 2, last, 0.0))
    ).astype(bf16)
    third = lane % E
    sign = jnp.where(third == expert_ref[0], 1.0, 0.0) - jnp.where(third == other, 1.0, 0.0)
    coef_ref[...] = jnp.where(lane < 3 * E, sign * both, 0.0)


def dx_kernel(place_ref, own_ref, core_ref, coef_ref, *refs):
    weights, (rows_ref, out_ref, three_ref, dp_ref) = side(refs[0:7]), refs[7:11]
    slots = own_ref.shape[0]
    rows = gathered_rows(rows_ref)
    width = rows.shape[1]

    @pl.when(pl.program_id(0) == 0)
    def _():
        def dp_of(ref):
            return jnp.sum(ref[:, 512:640].astype(f32), axis=1, keepdims=True)

        dp = dp_of(own_ref)
        coef = coef_ref[...] * (dp + dp_of(core_ref))
        hi, rest = split2(coef)
        lo, last = split2(rest)
        lane = iota((slots, 128), 1)
        three = jnp.where(lane < E, hi, jnp.where(lane < 2 * E, lo, last))
        three_ref[...] = three.T[0:32].astype(bf16)
        eye = iota((GROUP, 128), 0) == iota((GROUP, 128), 1)
        parts = []
        for i in range(M):
            for v in split2(dp[i * GROUP : (i + 1) * GROUP]):
                parts.append(jnp.sum(jnp.where(eye, v, 0.0), axis=0, keepdims=True))
        dp_ref[...] = jnp.concatenate(parts, axis=0)

    dims = (((1,), (1,)), ((), ()))
    dx = None
    for d_ref, start, part in zip(
        (own_ref, own_ref, core_ref, core_ref), (0, 256, 0, 256), weights
    ):
        d = d_ref[:, start : start + 256]
        got = lax.dot_general(d, part, dims, preferred_element_type=f32)
        dx = got if dx is None else dx + got
    got = jnp.dot(three_ref[...], rows, preferred_element_type=f32)
    router = got[0:E] + got[E : 2 * E] + got[2 * E : 3 * E]
    router_hi, router_lo = split2(router)
    for i in range(M):
        out_ref[i, 0:GROUP, :] = dx[i * GROUP : (i + 1) * GROUP].astype(bf16)
        dp_rows = jnp.concatenate(
            [dp_ref[2 * i : 2 * i + 2], jnp.zeros((2, width - 128), f32)], axis=1
        )
        meta = [router_hi[2 * i : 2 * i + 2], router_lo[2 * i : 2 * i + 2], dp_rows]
        meta = jnp.concatenate([*meta, jnp.zeros((2, width), f32)], axis=0)
        out_ref[i, GROUP:BLOCK, :] = meta.astype(bf16)


def sum_kernel(recv_ref, out_ref, acc_ref):
    step = pl.program_id(0)
    total = jnp.sum(recv_ref[...].astype(f32), axis=0)

    @pl.when(step == 0)
    def _():
        acc_ref[...] = total

    @pl.when(step != 0)
    def _():
        acc_ref[...] += total

    @pl.when(step == pl.num_programs(0) - 1)
    def _():
        meta = acc_ref[GROUP:BLOCK, :]
        router_hi, router_lo = split2(meta[0:2] + meta[2:4])
        dp_hi, dp_lo = split2(meta[4:5, 0:128] + meta[5:6, 0:128])
        dp_row = jnp.concatenate([jnp.zeros((1, 512), f32), dp_hi, dp_lo], axis=1)
        source = jnp.concatenate(
            [acc_ref[0:GROUP, :], router_hi, router_lo, dp_row, jnp.zeros((3, 768), f32)], axis=0
        ).astype(bf16)
        shape = (E * C * 8, BLOCK)
        column = iota(shape, 1)
        place, q = iota(shape, 0) // 8, iota(shape, 0) % 8
        hi, lo, dp = GROUP + place % 2, GROUP + 2 + place % 2, jnp.full(shape, GROUP + 4, i32)

        def pick_rows(cases):
            target = jnp.full(shape, -1, i32)
            for value, where in cases:
                target = jnp.where(q == value, where, target)
            return jnp.where(column == target, 1.0, 0.0).astype(bf16)

        slot = MOST * place
        first = pick_rows([(0, slot), (1, slot + 1), (2, slot + 2), (5, hi), (6, lo)])
        left = pick_rows([(3, slot), (4, slot + 2), (7, lo)])
        right = pick_rows([(3, slot + 1), (4, hi), (7, dp)])
        got = jnp.dot(first, source[:, 0:512], preferred_element_type=f32)
        tail = source[:, 512:768]
        out_ref[:, 0:256] = (
            got[:, 0:256] + jnp.dot(left, tail, preferred_element_type=f32)
        ).astype(bf16)
        out_ref[:, 256:512] = (
            got[:, 256:512] + jnp.dot(right, tail, preferred_element_type=f32)
        ).astype(bf16)


def call(kernel, grid, in_specs, out_specs, out_shape, scratch=(), limit=LIMIT):
    return pl.pallas_call(
        kernel,
        grid=grid,
        in_specs=in_specs,
        out_specs=out_specs,
        out_shape=out_shape,
        scratch_shapes=list(scratch),
        compiler_params=pltpu.CompilerParams(vmem_limit_bytes=limit),
    )


def placed(kernel, grid, in_specs, out_specs, out_shape, scratch=(), cost=None):
    return pl.pallas_call(
        kernel,
        grid_spec=pltpu.PrefetchScalarGridSpec(
            num_scalar_prefetch=1,
            grid=grid,
            in_specs=in_specs,
            out_specs=out_specs,
            scratch_shapes=list(scratch),
        ),
        out_shape=out_shape,
        compiler_params=pltpu.CompilerParams(vmem_limit_bytes=LIMIT),
        cost_estimate=cost,
    )


def whole(*shape):
    return pl.BlockSpec(shape, lambda *_: (0,) * len(shape))


def in_hbm(v):
    return pltpu.with_memory_space_constraint(v, HBM)


def a2a(v, axes):
    return lax.all_to_all(v, axes, split_axis=0, concat_axis=0, tiled=True)


def everywhere(v, count):
    return jnp.broadcast_to(v[None], (count,) + v.shape)


def swap(v):
    return lax.ppermute(v, "core", [(0, 1), (1, 0)])


def along_x(v):
    order = []
    for x in range(2 * X):
        for c in range(C):
            order.append((x * C + c, (x ^ 1 if c == 0 else 2 * X - 1 - x) * C + c))
    return lax.ppermute(v, ("xh", "xl", "core"), order)


def pick(v, index, axis):
    return lax.dynamic_index_in_dim(v, index, axis=axis, keepdims=False)


def local(tokens, routes, w_router, w_gate, w_up, cotangent):
    tok, width = tokens.shape
    half, piece = width // C, width // (C * Y)
    core, xl, sect = lax.axis_index("core"), lax.axis_index("xl"), lax.axis_index("sect")
    expert = lax.axis_index("e")
    slots = cotangent.shape[0] // 2
    sds = jax.ShapeDtypeStruct
    smem = pl.BlockSpec(memory_space=pltpu.SMEM)

    far_gate, far_up = along_x(w_gate), along_x(w_up)

    message, logits = call(
        route_kernel,
        (1,),
        [smem, smem, whole(tok, width), whole(E, width)],
        [whole(E, C, MOST + 1, piece), whole(tok, E)],
        [sds((E, C, MOST + 1, piece), bf16), sds((tok, E), f32)],
        limit=MOST_VMEM,
    )(sect.reshape(1).astype(i32), routes.T, tokens, w_router.T)
    arrived = a2a(message.reshape(E * C, MOST + 1, piece), ("e", "core"))

    place = core.reshape(1).astype(i32)

    def other_half(parts, cost=None):
        block = pl.BlockSpec((half, 128), lambda i, place: (1 - place[0], 0))
        return pl.pallas_call(
            half_kernel,
            grid_spec=pltpu.PrefetchScalarGridSpec(
                num_scalar_prefetch=1,
                grid=(1,),
                in_specs=[block] * len(parts),
                out_specs=whole(len(parts), half, 128),
            ),
            out_shape=sds((len(parts), half, 128), bf16),
            compiler_params=pltpu.CompilerParams(vmem_limit_bytes=LIMIT),
            cost_estimate=cost,
        )(place, *parts)

    near_other = other_half([w_gate, w_up])
    weights = (w_gate, w_up, far_gate, far_up, swap(near_other))
    weights += (swap(other_half([far_gate], LONG)), swap(other_half([far_up], LESS)))

    weights = [in_hbm(v) for v in weights]
    cot, _ = lax.optimization_barrier((cotangent, near_other))
    cot = cot.reshape(E, Z, X, 2, C * MOST, 128).transpose(3, 1, 2, 0, 4, 5)
    cot = cot.reshape(2, slots, 128)
    near_cot, far_cot = pick(cot, xl, 0), along_x(pick(cot, 1 - xl, 0))

    rows_spec = pl.BlockSpec((M, BLOCK, piece), lambda i: (i, 0, 0))
    gathered = call(
        gather_kernel,
        (Y,),
        [whole(E * C, MOST + 1, piece)],
        rows_spec,
        HBM((Y * M, BLOCK, piece), bf16),
        [pltpu.VMEM((BLOCK, piece), bf16)],
    )(arrived)
    rows = a2a(gathered, ("sect", "zl", "xh"))

    rows, near_cot, far_cot = lax.optimization_barrier((rows, near_cot, far_cot))

    def w_specs(rows, count):
        own = pl.BlockSpec((rows, 128), lambda i, place: (place[0] * count + i, 0))
        core = [pl.BlockSpec((n, rows, 128), lambda i, place: (0, i, 0)) for n in (2, 1, 1)]
        return [own] * 4 + core

    step_spec = pl.BlockSpec((M, BLOCK, piece), lambda i, place: (i, 0, 0))
    part = sds((slots, 512), f32)
    own, to_core = placed(
        pre_kernel,
        (1,),
        [whole(Y * M, BLOCK, piece)] + w_specs(half, 1),
        [whole(slots, 512), whole(slots, 512)],
        [part, part],
        [pltpu.VMEM((slots, half), bf16)],
    )(place, rows, *weights)
    hidden, far_hidden, d, coef = call(
        act_kernel,
        (1,),
        [smem]
        + [whole(slots, 512)] * 2
        + [whole(slots, 128)] * 2
        + [whole(M, BLOCK, piece)],
        [whole(slots, 128), whole(slots, 128), whole(slots, 640), whole(slots, 128)],
        [sds((slots, 128), bf16)] * 2 + [sds((slots, 640), bf16), sds((slots, 128), f32)],
    )(expert.reshape(1).astype(i32), own, swap(to_core), near_cot, far_cot, rows)

    back = placed(
        dx_kernel,
        (Y,),
        [whole(slots, 640)] * 2 + [whole(slots, 128)] + w_specs(piece, Y) + [step_spec],
        step_spec,
        HBM((Y * M, BLOCK, piece), bf16),
        [pltpu.VMEM((32, slots), bf16), pltpu.VMEM((2 * M, 128), f32)],
    )(place, d, swap(d), coef, *weights, rows)

    hidden_back = along_x(far_hidden)
    back = a2a(back, ("sect", "zl", "xh"))
    summed = call(
        sum_kernel,
        (Y,),
        [rows_spec],
        whole(E * C * 8, 512),
        sds((E * C * 8, 512), bf16),
        [pltpu.VMEM((BLOCK, piece), f32)],
    )(back)
    pairs = routes.reshape(-1)
    count = tok * 2
    same = pairs[:, None] == pairs[None, :]
    earlier = jnp.arange(count)[None, :] < jnp.arange(count)[:, None]
    ranks = jnp.sum((same & earlier).astype(i32), axis=1)
    places = pairs * MOST + ranks
    select = (places[None, :] == jnp.arange(E * MOST, dtype=i32)[:, None]).astype(f32)
    spread = jnp.sum(select.reshape(E * MOST, tok, 2), axis=2).astype(bf16)
    spread = spread.T.reshape(tok, E, MOST)
    choose = (routes[:, :, None] == jnp.arange(E, dtype=i32)[None, None, :]).astype(f32)
    probs = jax.nn.softmax(jnp.sum(choose * logits[:, None, :], axis=2), axis=1)
    w_mine = pick(w_router.reshape(C, Y, piece, E), sect, 1).astype(f32)

    summed, hidden_back, select, spread, choose, probs, w_mine = lax.optimization_barrier(
        (summed, hidden_back, select, spread, choose, probs, w_mine)
    )
    home = a2a(summed.reshape(E * C, 8, 512), ("e", "core"))
    home = home.reshape(E, C, 8, 512)

    mine = xl == jnp.arange(2)[:, None, None]
    hidden = jnp.where(mine, hidden[None], hidden_back[None])
    hidden = hidden.reshape(2, Z, X, E, C * MOST, 128).transpose(3, 1, 2, 0, 4, 5)
    hidden = hidden.reshape(2 * slots, 128)

    router_parts = jnp.concatenate(
        [
            home[:, :, 5, :].astype(f32) + home[:, :, 6, :].astype(f32),
            home[:, :, 4, 256:512].astype(f32) + home[:, :, 7, 0:256].astype(f32),
        ],
        axis=2,
    )
    router = jnp.sum(router_parts, axis=0).reshape(C * piece // 128, 128)
    router = a2a(everywhere(router, 2 * M * C), ("xl", "zl", "xh", "core"))

    tails = [home[:, :, 3, 0:256], home[:, :, 3, 256:512], home[:, :, 4, 0:256]]
    main = jnp.concatenate([home[:, :, 0:3, :], jnp.stack(tails, axis=2)], axis=3)
    token_dx = jnp.einsum("ter,ecrd->tcd", spread, main, preferred_element_type=f32)
    dp = jnp.sum(home[:, :, 7, 256:512].astype(f32), axis=1)
    dp = dp[:, 0:128] + dp[:, 128:256]
    dp = lax.dynamic_slice_in_dim(dp, (expert * C + core) * MOST, MOST, 1).reshape(E * MOST)
    pair_dp = jnp.sum(select * dp[:, None], axis=0).reshape(tok, 2)
    mean_dp = jnp.sum(probs * pair_dp, axis=1, keepdims=True)
    d_pick = probs * (pair_dp - mean_dp)
    d_logits = jnp.sum(choose * d_pick[:, :, None], axis=1)
    router_dx = jnp.einsum("te,cde->tcd", d_logits, w_mine, precision=lax.Precision.HIGHEST)
    grad_tokens = (token_dx + router_dx).astype(bf16).reshape(tok, C * piece)

    router = jnp.sum(router.reshape(2, E, C * piece), axis=0)
    hi = lax.reduce_precision(router, 8, 7)
    parts = [grad_tokens, hi.astype(bf16), (router - hi).astype(bf16)]
    got = a2a(everywhere(jnp.concatenate(parts, axis=0), Y), ("sect",))

    def whole_width(v):
        return v.reshape(Y, -1, C, piece).transpose(1, 2, 0, 3).reshape(-1, width)

    grad_tokens = whole_width(got[:, 0:tok])
    parts = got[:, tok:].astype(f32)
    grad_router = whole_width(parts[:, 0:E] + parts[:, E:])
    return hidden, grad_tokens, grad_router.T


def solution(mesh):
    fine = Mesh(mesh.devices.reshape(Y, E, Z, X, 2, C), AXES)
    seq = ("e", "zl", "xh", "xl", "core")
    columns = P(None, seq + ("sect",))
    return jax.shard_map(
        local,
        mesh=fine,
        in_specs=(P(seq, None), P(seq, None), P(), columns, columns, columns),
        out_specs=(columns, P(seq, None), P()),
        check_vma=False,
    )
```

time: 1370 us -> 165 us (0.12)
  waiting for transfers between devices: 1210 us -> 55.3 us
  starting transfers between devices: 40.7 us -> 76.8 us
  local copies, waits for them, and re-layouts: 42.8 us -> 8.2 us
  blocking collectives: 31.8 us -> 0 us
  Pallas kernels: 0 us -> 19.8 us
  matrix products: 19.3 us -> 0.46 us
    all_to_all x3 -> x6, waiting for transfers between devices: 831 us -> 44.8 us  [a2a(): return lax.all_to_all(v, axes, split_axis=0, concat_axis=0, tiled=True)]
    psum x2 -> x0, waiting for transfers between devices: 376 us -> none  [the longest x1 329 us: local(): grad_router = lax.psum(router_part, 'seq')]
    all_to_all x3 -> x0, local copies, waits for them, and re-layouts: 27.7 us -> none  [the longest x1 14.5 us: local(): lax.all_to_all(slot_dx, 'seq', split_axis=0, concat_axis=0, tiled=True)]
    ppermute x0 -> x9, starting transfers between devices: none -> 27.2 us  [the longest x4 16.3 us: along_x(): return lax.ppermute(v, ('xh', 'xl', 'core'), order)]
    all_to_all x1 -> x0, blocking collectives: 23 us -> none  [local(): lax.all_to_all(out_weights, 'seq', split_axis=0, concat_axis=0, tiled=True)]
    pallas_call x0 -> x9, Pallas kernels: none -> 19.8 us  [the longest x1 6.61 us: local(): placed(dx_kernel, (Y,), [whole(slots, 640)] * 2 + [whole(slots, 128)] + w...]
    dot_general x11 -> x2, matrix products: 19.3 us -> 0.46 us  [the longest x1 0.28 us: local(): jnp.einsum('ter,ecrd->tcd', spread, main, preferred_element_type=f32)]
    all_to_all x3 -> x6, starting transfers between devices: 40.6 us -> 49.6 us  [a2a(): return lax.all_to_all(v, axes, split_axis=0, concat_axis=0, tiled=True)]
  transfers between devices with their start and end apart: 5 -> 15, of which waited for: 5 -> 8; matrix products, arithmetic and copies ran while one was open for 0% -> 2% of each run, Pallas kernels for 0% -> 5%
where the time goes in v2:
time: 165 us; the launch traced here: 164 us
  starting transfers between devices  76.8 us (47%)
  waiting for transfers between devices  55.3 us (34%)
  Pallas kernels  19.8 us (12%)
  local copies, waits for them, and re-layouts  8.2 us (5%)
  other arithmetic  2.59 us (2%)
    all_to_all x6, starting transfers between devices, a2a(): return lax.all_to_all(v, axes, split_axis=0, concat_axis=0, tiled=True)  49.6 us
    all_to_all x6, waiting for transfers between devices, a2a(): return lax.all_to_all(v, axes, split_axis=0, concat_axis=0, tiled=True)  44.8 us
    ppermute x4, starting transfers between devices, along_x(): return lax.ppermute(v, ('xh', 'xl', 'core'), order)  16.3 us
    ppermute x5, starting transfers between devices, swap(): return lax.ppermute(v, 'core', [(0, 1), (1, 0)])  10.9 us
    ppermute x4, waiting for transfers between devices, along_x(): return lax.ppermute(v, ('xh', 'xl', 'core'), order)  8.14 us
    pallas_call x1, Pallas kernels, local(): placed(dx_kernel, (Y,), [whole(slots, 640)] * 2 + [whole(slots, 128)] + w...  6.61 us
    pallas_call x1, Pallas kernels, local(): placed(pre_kernel, (1,), [whole(Y * M, BLOCK, piece)] + w_specs(half, 1),...  4.17 us
    pallas_call x3, Pallas kernels, other_half(): pl.pallas_call(half_kernel, grid_spec=pltpu.PrefetchScalarGridSpec(num_sc...  3.49 us
  transfers between devices with their start and end apart: 15, of which 8 were waited for; matrix products, arithmetic and copies ran while one was open for 2% of the time, Pallas kernels for 5%

profile of v2, /device:TPU:1, one launch (start us, length us, event | category | flops | bytes accessed | tf_op | source)
XLA Modules:
  0.0 164.4 jit_solution(15416263211171582968)
XLA Ops:
  0.6 5.2 %collective-permute-start.1 = (bf16[6144,128]{1,0:T(8,128)(2,1)}, bf16[6144,128]{1,0:T(8,128)(2,1)S(1)}, u32[]{:S(2)}, u32[]{:S(2)}) collective-permute-start(bf16[6144,128]{1,0:T(8,128)(2,1)} %refs_0_.5), channel_id=1, source_target_pairs={{0,2},{1,7},{2,0},{3,5},{4,6},{5,3},{6,4},{7,1},{8,10},{9,15},{10,... | collective-permute-start | bytes 4718600 | tf_op jit(solution)/shard_map/ppermute | solution.py:326
  5.9 2.1 %shard_map.85 = (bf16[8,2,4,768]{3,2,1,0:T(4,128)(2,1)}, f32[8,8]{1,0:T(8,128)}) custom-call(s32[1]{0:T(128)} %bitcast.2.place_ref, s32[2,8]{1,0:T(2,128)} %bitcast.68, bf16[8,6144]{1,0:T(8,128)(2,1)} %tokens_ref.1, bf16[8,6144]{1,0:T(8,128)(2,1)} %bitcast.61), custom_call_target="tpu_custom_call" | custom-call | tf_op jit(solution)/shard_map/pallas_call | solution.py:344
  7.9 15.2 %all-to-all-start = ((bf16[16,4,768]{2,1,0:T(4,128)(2,1)}), bf16[16,4,768]{2,1,0:T(4,128)(2,1)S(1)}, u32[]{:S(2)}, u32[]{:S(2)}) async-start(bf16[16,4,768]{2,1,0:T(4,128)(2,1)} %bitcast.64), calls=%async_computation | async-start | bytes 196608 | tf_op jit(solution)/shard_map/all_to_all | solution.py:310
  23.2 3.3 %collective-permute-start.2 = (bf16[6144,128]{1,0:T(8,128)(2,1)}, bf16[6144,128]{1,0:T(8,128)(2,1)}, u32[]{:S(2)}, u32[]{:S(2)}) collective-permute-start(bf16[6144,128]{1,0:T(8,128)(2,1)} %refs_1_.5), channel_id=1, source_target_pairs={{0,2},{1,7},{2,0},{3,5},{4,6},{5,3},{6,4},{7,1},{8,10},{9,15},{10,... | collective-permute-start | bytes 4718600 | tf_op jit(solution)/shard_map/ppermute | solution.py:326
  26.5 1.4 copy-done
  27.9 1.4 copy-done.1
  29.3 1.3 shard_map.87
  30.5 1.9 %collective-permute-start.3 = (bf16[2,3072,128]{2,1,0:T(8,128)(2,1)}, bf16[2,3072,128]{2,1,0:T(8,128)(2,1)}, u32[]{:S(2)}, u32[]{:S(2)}) collective-permute-start(bf16[2,3072,128]{2,1,0:T(8,128)(2,1)} %shard_map.87), channel_id=1, source_target_pairs={{0,1},{1,0},{2,3},{3,2},{4,5},{5,4},{6,7},{7,6},{8,9},{9,8},{10,11... | collective-permute-start | bytes 4718600 | tf_op jit(solution)/shard_map/ppermute | solution.py:318
  32.5 5.3 %all-to-all-done.arrived_ref = bf16[16,4,768]{2,1,0:T(4,128)(2,1)S(1)} async-done(((bf16[16,4,768]{2,1,0:T(4,128)(2,1)}), bf16[16,4,768]{2,1,0:T(4,128)(2,1)S(1)}, u32[]{:S(2)}, u32[]{:S(2)}) %all-to-all-start) | async-done | bytes 98336 | tf_op jit(solution)/shard_map/all_to_all | solution.py:310
  37.7 1.9 %shard_map.86 = bf16[16,56,768]{2,1,0:T(8,128)(2,1)} custom-call(bf16[16,4,768]{2,1,0:T(4,128)(2,1)S(1)} %all-to-all-done.arrived_ref), custom_call_target="tpu_custom_call" | custom-call | tf_op jit(solution)/shard_map/pallas_call | solution.py:382
  39.6 6.0 %all-to-all-start.1 = ((bf16[16,56,768]{2,1,0:T(8,128)(2,1)}), bf16[16,56,768]{2,1,0:T(8,128)(2,1)S(1)}, u32[]{:S(2)}, u32[]{:S(2)}) async-start(bf16[16,56,768]{2,1,0:T(8,128)(2,1)} %shard_map.86), calls=%async_computation.1 | async-start | bytes 2752512 | tf_op jit(solution)/shard_map/all_to_all | solution.py:310
  47.1 2.0 %collective-permute-start.4 = (bf16[1,3072,128]{2,1,0:T(8,128)(2,1)}, bf16[1,3072,128]{2,1,0:T(8,128)(2,1)}, u32[]{:S(2)}, u32[]{:S(2)}) collective-permute-start(bf16[1,3072,128]{2,1,0:T(8,128)(2,1)} %shard_map.88), channel_id=1, source_target_pairs={{0,1},{1,0},{2,3},{3,2},{4,5},{5,4},{6,7},{7,6},{8,9},{9,8},{10,11... | collective-permute-start | bytes 2359304 | tf_op jit(solution)/shard_map/ppermute | solution.py:318
  49.2 1.2 shard_map.89
  50.4 2.4 %collective-permute-start.5 = (bf16[1,3072,128]{2,1,0:T(8,128)(2,1)S(1)}, bf16[1,3072,128]{2,1,0:T(8,128)(2,1)}, u32[]{:S(2)}, u32[]{:S(2)}) collective-permute-start(bf16[1,3072,128]{2,1,0:T(8,128)(2,1)S(1)} %shard_map.89), channel_id=1, source_target_pairs={{0,1},{1,0},{2,3},{3,2},{4,5},{5,4},{6,7},{7,6},{8,9},{9,8},{10,11... | collective-permute-start | bytes 2359304 | tf_op jit(solution)/shard_map/ppermute | solution.py:318
  53.2 4.1 %collective-permute-start = (bf16[192,128]{1,0:T(8,128)(2,1)S(1)}, bf16[192,128]{1,0:T(8,128)(2,1)S(1)}, u32[]{:S(2)}, u32[]{:S(2)}) collective-permute-start(bf16[192,128]{1,0:T(8,128)(2,1)S(1)} %bitcast.67), channel_id=1, source_target_pairs={{0,2},{1,7},{2,0},{3,5},{4,6},{5,3},{6,4},{7,1},{8,10},{9,15},{10,... | collective-permute-start | bytes 147464 | tf_op jit(solution)/shard_map/ppermute | solution.py:326
  57.3 8.1 %collective-permute-done.far_cot_ref = bf16[192,128]{1,0:T(8,128)(2,1)S(1)} collective-permute-done((bf16[192,128]{1,0:T(8,128)(2,1)S(1)}, bf16[192,128]{1,0:T(8,128)(2,1)S(1)}, u32[]{:S(2)}, u32[]{:S(2)}) %collective-permute-start) | collective-permute-done | bytes 49184 | tf_op jit(solution)/shard_map/ppermute | solution.py:326
  65.5 4.2 %shard_map.90 = (f32[192,512]{1,0:T(8,128)S(1)}, f32[192,512]{1,0:T(8,128)S(1)}) custom-call(s32[1]{0:T(128)} %bitcast.1.place_ref, bf16[16,56,768]{2,1,0:T(8,128)(2,1)S(1)} %all-to-all-done.1.rows_ref.refs_7_, bf16[6144,128]{1,0:T(8,128)(2,1)} %refs_0_.5, bf16[6144,128]{1,0:T(8,128)(2,1)} %refs_1_.5, bf16[6144,128]{1,0:T(8,128)(2,1)} %copy-done.2, ...), custom_call_target="tpu_custom_call" | custom-call | tf_op jit(solution)/shard_map/pallas_call | solution.py:401
  69.7 2.3 %collective-permute-start.6 = (f32[192,512]{1,0:T(8,128)S(1)}, f32[192,512]{1,0:T(8,128)S(1)}, u32[]{:S(2)}, u32[]{:S(2)}) collective-permute-start(f32[192,512]{1,0:T(8,128)S(1)} %get-tuple-element.26), channel_id=1, source_target_pairs={{0,1},{1,0},{2,3},{3,2},{4,5},{5,4},{6,7},{7,6},{8,9},{9,8},{10,11... | collective-permute-start | bytes 1179656 | tf_op jit(solution)/shard_map/ppermute | solution.py:318
  72.0 1.3 collective-permute-done.6.core_ref
  73.7 2.3 %collective-permute-start.7 = (bf16[192,640]{1,0:T(8,128)(2,1)S(1)}, bf16[192,640]{1,0:T(8,128)(2,1)S(1)}, u32[]{:S(2)}, u32[]{:S(2)}) collective-permute-start(bf16[192,640]{1,0:T(8,128)(2,1)S(1)} %get-tuple-element.30.own_ref), channel_id=1, source_target_pairs={{0,1},{1,0},{2,3},{3,2},{4,5},{5,4},{6,7},{7,6},{8,9},{9,8},{10,11... | collective-permute-start | bytes 737288 | tf_op jit(solution)/shard_map/ppermute | solution.py:318
  76.0 1.1 collective-permute-done.7.core_ref
  77.1 6.6 %shard_map.92 = bf16[16,56,768]{2,1,0:T(8,128)(2,1)} custom-call(s32[1]{0:T(128)} %bitcast.1.place_ref, bf16[192,640]{1,0:T(8,128)(2,1)S(1)} %get-tuple-element.30.own_ref, bf16[192,640]{1,0:T(8,128)(2,1)S(1)} %collective-permute-done.7.core_ref, f32[192,128]{1,0:T(8,128)S(1)} %get-tuple-element.31.coef_ref, bf16[6144,128]{1,0:T(8,128)(2,1)} %refs_0_.5, ...), custom_call_target="tpu_custom_call" | custom-call | tf_op jit(solution)/shard_map/pallas_call | solution.py:420
  83.8 7.0 %all-to-all-start.2 = ((bf16[16,56,768]{2,1,0:T(8,128)(2,1)}), bf16[16,56,768]{2,1,0:T(8,128)(2,1)S(1)}, u32[]{:S(2)}, u32[]{:S(2)}) async-start(bf16[16,56,768]{2,1,0:T(8,128)(2,1)} %shard_map.92), calls=%async_computation.2 | async-start | bytes 2752512 | tf_op jit(solution)/shard_map/all_to_all | solution.py:310
  91.8 3.7 %collective-permute-start.8 = (bf16[192,128]{1,0:T(8,128)(2,1)S(1)}, bf16[192,128]{1,0:T(8,128)(2,1)S(1)}, u32[]{:S(2)}, u32[]{:S(2)}) collective-permute-start(bf16[192,128]{1,0:T(8,128)(2,1)S(1)} %get-tuple-element.32), channel_id=1, source_target_pairs={{0,2},{1,7},{2,0},{3,5},{4,6},{5,3},{6,4},{7,1},{8,10},{9,15},{10,... | collective-permute-start | bytes 147464 | tf_op jit(solution)/shard_map/ppermute | solution.py:326
  96.3 13.1 %all-to-all-done.2.recv_ref = bf16[16,56,768]{2,1,0:T(8,128)(2,1)S(1)} async-done(((bf16[16,56,768]{2,1,0:T(8,128)(2,1)}), bf16[16,56,768]{2,1,0:T(8,128)(2,1)S(1)}, u32[]{:S(2)}, u32[]{:S(2)}) %all-to-all-start.2) | async-done | bytes 1376288 | tf_op jit(solution)/shard_map/all_to_all | solution.py:310
  109.4 1.2 shard_map.93
  110.7 13.1 %all-to-all-start.3 = ((bf16[16,8,512]{2,1,0:T(8,128)(2,1)}), bf16[16,8,512]{2,1,0:T(8,128)(2,1)S(1)}, u32[]{:S(2)}, u32[]{:S(2)}) async-start(bf16[16,8,512]{2,1,0:T(8,128)(2,1)} %bitcast.14), calls=%async_computation.3 | async-start | bytes 262144 | tf_op jit(solution)/shard_map/all_to_all | solution.py:310
  124.4 15.3 %all-to-all-done.3 = bf16[16,8,512]{2,1,0:T(8,128)(2,1)S(1)} async-done(((bf16[16,8,512]{2,1,0:T(8,128)(2,1)}), bf16[16,8,512]{2,1,0:T(8,128)(2,1)S(1)}, u32[]{:S(2)}, u32[]{:S(2)}) %all-to-all-start.3) | async-done | bytes 131104 | tf_op jit(solution)/shard_map/all_to_all | solution.py:310
  141.1 4.7 %all-to-all-start.4 = ((f32[16,12,128]{2,1,0:T(8,128)}), f32[16,12,128]{2,1,0:T(8,128)S(1)}, u32[]{:S(2)}, u32[]{:S(2)}) async-start(f32[16,12,128]{2,1,0:T(8,128)} %broadcast_in_dim.79), calls=%async_computation.4 | async-start | bytes 262144 | tf_op jit(solution)/shard_map/all_to_all | solution.py:310
  146.5 5.5 %all-to-all-done.4 = f32[16,12,128]{2,1,0:T(8,128)S(1)} async-done(((f32[16,12,128]{2,1,0:T(8,128)}), f32[16,12,128]{2,1,0:T(8,128)S(1)}, u32[]{:S(2)}, u32[]{:S(2)}) %all-to-all-start.4) | async-done | bytes 98336 | tf_op jit(solution)/shard_map/all_to_all | solution.py:310
  152.8 3.5 %all-to-all-start.5 = ((bf16[4,24,1536]{2,1,0:T(8,128)(2,1)}), bf16[4,24,1536]{2,1,0:T(8,128)(2,1)S(1)}, u32[]{:S(2)}, u32[]{:S(2)}) async-start(bf16[4,24,1536]{2,1,0:T(8,128)(2,1)} %broadcast_in_dim.80), calls=%async_computation.5 | async-start | bytes 589824 | tf_op jit(solution)/shard_map/all_to_all | solution.py:310
  157.0 5.5 %all-to-all-done.5 = bf16[4,24,1536]{2,1,0:T(8,128)(2,1)S(1)} async-done(((bf16[4,24,1536]{2,1,0:T(8,128)(2,1)}), bf16[4,24,1536]{2,1,0:T(8,128)(2,1)S(1)}, u32[]{:S(2)}, u32[]{:S(2)}) %all-to-all-start.5) | async-done | bytes 294944 | tf_op jit(solution)/shard_map/all_to_all | solution.py:310
  (92 shorter events, 9.9 us)
Async XLA Ops:
  0.6 45.1 %collective-permute-start.1 = (bf16[6144,128]{1,0:T(8,128)(2,1)}, bf16[6144,128]{1,0:T(8,128)(2,1)S(1)}, u32[]{:S(2)}, u32[]{:S(2)}) collective-permute-start(bf16[6144,128]{1,0:T(8,128)(2,1)} %refs_0_.5), channel_id=1, source_target_pairs={{0,2},{1,7},{2,0},{3,5},{4,6},{5,3},{6,4},{7,1},{8,10},{9,15},{10,... | collective-permute-start | bytes 4718600 | tf_op jit(solution)/shard_map/ppermute | solution.py:326
  7.9 29.8 %all-to-all-start = ((bf16[16,4,768]{2,1,0:T(4,128)(2,1)}), bf16[16,4,768]{2,1,0:T(4,128)(2,1)S(1)}, u32[]{:S(2)}, u32[]{:S(2)}) async-start(bf16[16,4,768]{2,1,0:T(4,128)(2,1)} %bitcast.64), calls=%async_computation | async-start | bytes 196608 | tf_op jit(solution)/shard_map/all_to_all | solution.py:310
  23.2 26.0 %collective-permute-start.2 = (bf16[6144,128]{1,0:T(8,128)(2,1)}, bf16[6144,128]{1,0:T(8,128)(2,1)}, u32[]{:S(2)}, u32[]{:S(2)}) collective-permute-start(bf16[6144,128]{1,0:T(8,128)(2,1)} %refs_1_.5), channel_id=1, source_target_pairs={{0,2},{1,7},{2,0},{3,5},{4,6},{5,3},{6,4},{7,1},{8,10},{9,15},{10,... | collective-permute-start | bytes 4718600 | tf_op jit(solution)/shard_map/ppermute | solution.py:326
  26.5 1.4 copy-start
  27.9 1.4 copy-start.1
  30.5 35.0 %collective-permute-start.3 = (bf16[2,3072,128]{2,1,0:T(8,128)(2,1)}, bf16[2,3072,128]{2,1,0:T(8,128)(2,1)}, u32[]{:S(2)}, u32[]{:S(2)}) collective-permute-start(bf16[2,3072,128]{2,1,0:T(8,128)(2,1)} %shard_map.87), channel_id=1, source_target_pairs={{0,1},{1,0},{2,3},{3,2},{4,5},{5,4},{6,7},{7,6},{8,9},{9,8},{10,11... | collective-permute-start | bytes 4718600 | tf_op jit(solution)/shard_map/ppermute | solution.py:318
  39.6 25.9 %all-to-all-start.1 = ((bf16[16,56,768]{2,1,0:T(8,128)(2,1)}), bf16[16,56,768]{2,1,0:T(8,128)(2,1)S(1)}, u32[]{:S(2)}, u32[]{:S(2)}) async-start(bf16[16,56,768]{2,1,0:T(8,128)(2,1)} %shard_map.86), calls=%async_computation.1 | async-start | bytes 2752512 | tf_op jit(solution)/shard_map/all_to_all | solution.py:310
  45.7 1.4 copy-start.2
  47.1 5.7 %copy-start.3 = (bf16[384,128]{1,0:T(8,128)(2,1)S(1)}, bf16[384,128]{1,0:T(8,128)(2,1)}, u32[]{:S(2)}) copy-start(bf16[384,128]{1,0:T(8,128)(2,1)} %param.11) | copy-start | bytes 294916
  47.1 18.4 %collective-permute-start.4 = (bf16[1,3072,128]{2,1,0:T(8,128)(2,1)}, bf16[1,3072,128]{2,1,0:T(8,128)(2,1)}, u32[]{:S(2)}, u32[]{:S(2)}) collective-permute-start(bf16[1,3072,128]{2,1,0:T(8,128)(2,1)} %shard_map.88), channel_id=1, source_target_pairs={{0,1},{1,0},{2,3},{3,2},{4,5},{5,4},{6,7},{7,6},{8,9},{9,8},{10,11... | collective-permute-start | bytes 2359304 | tf_op jit(solution)/shard_map/ppermute | solution.py:318
  50.4 15.1 %collective-permute-start.5 = (bf16[1,3072,128]{2,1,0:T(8,128)(2,1)S(1)}, bf16[1,3072,128]{2,1,0:T(8,128)(2,1)}, u32[]{:S(2)}, u32[]{:S(2)}) collective-permute-start(bf16[1,3072,128]{2,1,0:T(8,128)(2,1)S(1)} %shard_map.89), channel_id=1, source_target_pairs={{0,1},{1,0},{2,3},{3,2},{4,5},{5,4},{6,7},{7,6},{8,9},{9,8},{10,11... | collective-permute-start | bytes 2359304 | tf_op jit(solution)/shard_map/ppermute | solution.py:318
  53.2 12.3 %collective-permute-start = (bf16[192,128]{1,0:T(8,128)(2,1)S(1)}, bf16[192,128]{1,0:T(8,128)(2,1)S(1)}, u32[]{:S(2)}, u32[]{:S(2)}) collective-permute-start(bf16[192,128]{1,0:T(8,128)(2,1)S(1)} %bitcast.67), channel_id=1, source_target_pairs={{0,2},{1,7},{2,0},{3,5},{4,6},{5,3},{6,4},{7,1},{8,10},{9,15},{10,... | collective-permute-start | bytes 147464 | tf_op jit(solution)/shard_map/ppermute | solution.py:326
  69.7 3.6 %collective-permute-start.6 = (f32[192,512]{1,0:T(8,128)S(1)}, f32[192,512]{1,0:T(8,128)S(1)}, u32[]{:S(2)}, u32[]{:S(2)}) collective-permute-start(f32[192,512]{1,0:T(8,128)S(1)} %get-tuple-element.26), channel_id=1, source_target_pairs={{0,1},{1,0},{2,3},{3,2},{4,5},{5,4},{6,7},{7,6},{8,9},{9,8},{10,11... | collective-permute-start | bytes 1179656 | tf_op jit(solution)/shard_map/ppermute | solution.py:318
  73.7 3.4 %collective-permute-start.7 = (bf16[192,640]{1,0:T(8,128)(2,1)S(1)}, bf16[192,640]{1,0:T(8,128)(2,1)S(1)}, u32[]{:S(2)}, u32[]{:S(2)}) collective-permute-start(bf16[192,640]{1,0:T(8,128)(2,1)S(1)} %get-tuple-element.30.own_ref), channel_id=1, source_target_pairs={{0,1},{1,0},{2,3},{3,2},{4,5},{5,4},{6,7},{7,6},{8,9},{9,8},{10,11... | collective-permute-start | bytes 737288 | tf_op jit(solution)/shard_map/ppermute | solution.py:318
  83.7 7.0 %copy-start.4 = (s32[8,2]{0,1:T(2,128)S(1)}, s32[8,2]{0,1:T(2,128)}, u32[]{:S(2)}) copy-start(s32[8,2]{0,1:T(2,128)} %param.7) | copy-start | bytes 196
  83.8 7.6 %copy-start.5 = (f32[8,8]{1,0:T(8,128)S(1)}, f32[8,8]{1,0:T(8,128)}, u32[]{:S(2)}) copy-start(f32[8,8]{1,0:T(8,128)} %get-tuple-element.33) | copy-start | bytes 772
  83.8 25.7 %all-to-all-start.2 = ((bf16[16,56,768]{2,1,0:T(8,128)(2,1)}), bf16[16,56,768]{2,1,0:T(8,128)(2,1)S(1)}, u32[]{:S(2)}, u32[]{:S(2)}) async-start(bf16[16,56,768]{2,1,0:T(8,128)(2,1)} %shard_map.92), calls=%async_computation.2 | async-start | bytes 2752512 | tf_op jit(solution)/shard_map/all_to_all | solution.py:310
  91.8 18.9 %collective-permute-start.8 = (bf16[192,128]{1,0:T(8,128)(2,1)S(1)}, bf16[192,128]{1,0:T(8,128)(2,1)S(1)}, u32[]{:S(2)}, u32[]{:S(2)}) collective-permute-start(bf16[192,128]{1,0:T(8,128)(2,1)S(1)} %get-tuple-element.32), channel_id=1, source_target_pairs={{0,2},{1,7},{2,0},{3,5},{4,6},{5,3},{6,4},{7,1},{8,10},{9,15},{10,... | collective-permute-start | bytes 147464 | tf_op jit(solution)/shard_map/ppermute | solution.py:326
  110.7 29.0 %all-to-all-start.3 = ((bf16[16,8,512]{2,1,0:T(8,128)(2,1)}), bf16[16,8,512]{2,1,0:T(8,128)(2,1)S(1)}, u32[]{:S(2)}, u32[]{:S(2)}) async-start(bf16[16,8,512]{2,1,0:T(8,128)(2,1)} %bitcast.14), calls=%async_computation.3 | async-start | bytes 262144 | tf_op jit(solution)/shard_map/all_to_all | solution.py:310
  141.1 10.9 %all-to-all-start.4 = ((f32[16,12,128]{2,1,0:T(8,128)}), f32[16,12,128]{2,1,0:T(8,128)S(1)}, u32[]{:S(2)}, u32[]{:S(2)}) async-start(f32[16,12,128]{2,1,0:T(8,128)} %broadcast_in_dim.79), calls=%async_computation.4 | async-start | bytes 262144 | tf_op jit(solution)/shard_map/all_to_all | solution.py:310
  152.8 9.7 %all-to-all-start.5 = ((bf16[4,24,1536]{2,1,0:T(8,128)(2,1)}), bf16[4,24,1536]{2,1,0:T(8,128)(2,1)S(1)}, u32[]{:S(2)}, u32[]{:S(2)}) async-start(bf16[4,24,1536]{2,1,0:T(8,128)(2,1)} %broadcast_in_dim.80), calls=%async_computation.5 | async-start | bytes 589824 | tf_op jit(solution)/shard_map/all_to_all | solution.py:310

commit v3 on v2

--- a/solution.py
+++ b/solution.py
@@ -270,6 +270,41 @@
         ).astype(bf16)
 
 
+def router_kernel(home_ref, out_ref):
+    rows = []
+    for c in range(C):
+        total = home_ref[c].astype(f32)
+        for e in range(1, E):
+            total = total + home_ref[e * C + c].astype(f32)
+        rest = total[4:5, 256:512] + total[7:8, 0:256]
+        rows.append(jnp.concatenate([total[5:6] + total[6:7], rest], axis=1))
+    rows = jnp.concatenate(rows, axis=0)
+    for i in range(out_ref.shape[0]):
+        out_ref[i] = rows
+
+
+def pack_kernel(tokens_ref, router_ref, out_ref):
+    piece = router_ref.shape[2]
+    for c in range(C):
+        part = slice(c * piece, (c + 1) * piece)
+        total = router_ref[0:E, c, :] + router_ref[E : 2 * E, c, :]
+        hi, lo = split2(total)
+        block = jnp.concatenate([tokens_ref[:, part].astype(f32), hi, lo], axis=0).astype(bf16)
+        for y in range(Y):
+            out_ref[y, :, part] = block
+
+
+def last_kernel(got_ref, tokens_ref, router_ref):
+    tok = tokens_ref.shape[0]
+    piece = got_ref.shape[2] // C
+    for y in range(Y):
+        for c in range(C):
+            block = got_ref[y, :, c * piece : (c + 1) * piece].astype(f32)
+            part = slice((c * Y + y) * piece, (c * Y + y + 1) * piece)
+            tokens_ref[:, part] = block[0:tok].astype(bf16)
+            router_ref[:, part] = block[tok : tok + E] + block[tok + E :]
+
+
 def call(kernel, grid, in_specs, out_specs, out_shape, scratch=(), limit=LIMIT):
     return pl.pallas_call(
         kernel,
@@ -460,15 +495,14 @@
     hidden = hidden.reshape(2, Z, X, E, C * MOST, 128).transpose(3, 1, 2, 0, 4, 5)
     hidden = hidden.reshape(2 * slots, 128)
 
-    router_parts = jnp.concatenate(
-        [
-            home[:, :, 5, :].astype(f32) + home[:, :, 6, :].astype(f32),
-            home[:, :, 4, 256:512].astype(f32) + home[:, :, 7, 0:256].astype(f32),
-        ],
-        axis=2,
-    )
-    router = jnp.sum(router_parts, axis=0).reshape(C * piece // 128, 128)
-    router = a2a(everywhere(router, 2 * M * C), ("xl", "zl", "xh", "core"))
+    router = call(
+        router_kernel,
+        (1,),
+        [whole(E * C, 8, 512)],
+        whole(2 * M * C, C, piece),
+        sds((2 * M * C, C, piece), f32),
+    )(home.reshape(E * C, 8, 512))
+    router = a2a(router, ("xl", "zl", "xh", "core"))
 
     tails = [home[:, :, 3, 0:256], home[:, :, 3, 256:512], home[:, :, 4, 0:256]]
     main = jnp.concatenate([home[:, :, 0:3, :], jnp.stack(tails, axis=2)], axis=3)
@@ -483,17 +517,20 @@
     router_dx = jnp.einsum("te,cde->tcd", d_logits, w_mine, precision=lax.Precision.HIGHEST)
     grad_tokens = (token_dx + router_dx).astype(bf16).reshape(tok, C * piece)
 
-    router = jnp.sum(router.reshape(2, E, C * piece), axis=0)
-    hi = lax.reduce_precision(router, 8, 7)
-    parts = [grad_tokens, hi.astype(bf16), (router - hi).astype(bf16)]
-    got = a2a(everywhere(jnp.concatenate(parts, axis=0), Y), ("sect",))
-
-    def whole_width(v):
-        return v.reshape(Y, -1, C, piece).transpose(1, 2, 0, 3).reshape(-1, width)
-
-    grad_tokens = whole_width(got[:, 0:tok])
-    parts = got[:, tok:].astype(f32)
-    grad_router = whole_width(parts[:, 0:E] + parts[:, E:])
+    packed = call(
+        pack_kernel,
+        (1,),
+        [whole(tok, C * piece), whole(2 * E, C, piece)],
+        whole(Y, tok + 2 * E, C * piece),
+        sds((Y, tok + 2 * E, C * piece), bf16),
+    )(grad_tokens, router)
+    grad_tokens, grad_router = call(
+        last_kernel,
+        (1,),
+        [whole(Y, tok + 2 * E, C * piece)],
+        [whole(tok, width), whole(E, width)],
+        [sds((tok, width), bf16), sds((E, width), f32)],
+    )(a2a(packed, ("sect",)))
     return hidden, grad_tokens, grad_router.T
 
 

time: 165 us -> 164 us (level)
  local copies, waits for them, and re-layouts: 8.2 us -> 4.92 us
  Pallas kernels: 19.8 us -> 22 us
    pallas_call x0 -> x3, Pallas kernels: none -> 2.22 us  [the longest x1 0.81 us: local(): call(pack_kernel, (1,), [whole(tok, C * piece), whole(2 * E, C, piece)],...]
    unnamed x21 -> x19, local copies, waits for them, and re-layouts: 3.38 us -> 3.34 us
where the time goes in v3:
time: 164 us; the launch traced here: 163 us
  starting transfers between devices  76.8 us (47%)
  waiting for transfers between devices  55.2 us (34%)
  Pallas kernels  22 us (13%)
  local copies, waits for them, and re-layouts  4.92 us (3%)
  other arithmetic  2.4 us (1%)
    all_to_all x6, starting transfers between devices, a2a(): return lax.all_to_all(v, axes, split_axis=0, concat_axis=0, tiled=True)  49.6 us
    all_to_all x6, waiting for transfers between devices, a2a(): return lax.all_to_all(v, axes, split_axis=0, concat_axis=0, tiled=True)  44.6 us
    ppermute x4, starting transfers between devices, along_x(): return lax.ppermute(v, ('xh', 'xl', 'core'), order)  16.3 us
    ppermute x5, starting transfers between devices, swap(): return lax.ppermute(v, 'core', [(0, 1), (1, 0)])  10.9 us
    ppermute x4, waiting for transfers between devices, along_x(): return lax.ppermute(v, ('xh', 'xl', 'core'), order)  8.16 us
    pallas_call x1, Pallas kernels, local(): placed(dx_kernel, (Y,), [whole(slots, 640)] * 2 + [whole(slots, 128)] + w...  6.63 us
    pallas_call x1, Pallas kernels, local(): placed(pre_kernel, (1,), [whole(Y * M, BLOCK, piece)] + w_specs(half, 1),...  4.18 us
    pallas_call x3, Pallas kernels, other_half(): pl.pallas_call(half_kernel, grid_spec=pltpu.PrefetchScalarGridSpec(num_sc...  3.47 us
  transfers between devices with their start and end apart: 15, of which 8 were waited for; matrix products, arithmetic and copies ran while one was open for 2% of the time, Pallas kernels for 5%

profile of v3, /device:TPU:1, one launch (start us, length us, event | category | flops | bytes accessed | tf_op | source)
XLA Modules:
  0.0 162.9 jit_solution(1633581320091806639)
XLA Ops:
  0.6 5.2 %collective-permute-start.1 = (bf16[6144,128]{1,0:T(8,128)(2,1)}, bf16[6144,128]{1,0:T(8,128)(2,1)S(1)}, u32[]{:S(2)}, u32[]{:S(2)}) collective-permute-start(bf16[6144,128]{1,0:T(8,128)(2,1)} %refs_0_.5), channel_id=1, source_target_pairs={{0,2},{1,7},{2,0},{3,5},{4,6},{5,3},{6,4},{7,1},{8,10},{9,15},{10,... | collective-permute-start | bytes 4718600 | tf_op jit(solution)/shard_map/ppermute | solution.py:361
  5.9 2.1 %shard_map.85 = (bf16[8,2,4,768]{3,2,1,0:T(4,128)(2,1)}, f32[8,8]{1,0:T(8,128)}) custom-call(s32[1]{0:T(128)} %bitcast.2.place_ref, s32[2,8]{1,0:T(2,128)} %bitcast.54, bf16[8,6144]{1,0:T(8,128)(2,1)} %tokens_ref.1, bf16[8,6144]{1,0:T(8,128)(2,1)} %bitcast.50), custom_call_target="tpu_custom_call" | custom-call | tf_op jit(solution)/shard_map/pallas_call | solution.py:379
  7.9 15.2 %all-to-all-start = ((bf16[16,4,768]{2,1,0:T(4,128)(2,1)}), bf16[16,4,768]{2,1,0:T(4,128)(2,1)S(1)}, u32[]{:S(2)}, u32[]{:S(2)}) async-start(bf16[16,4,768]{2,1,0:T(4,128)(2,1)} %bitcast.52), calls=%async_computation | async-start | bytes 196608 | tf_op jit(solution)/shard_map/all_to_all | solution.py:345
  23.2 3.3 %collective-permute-start.2 = (bf16[6144,128]{1,0:T(8,128)(2,1)}, bf16[6144,128]{1,0:T(8,128)(2,1)}, u32[]{:S(2)}, u32[]{:S(2)}) collective-permute-start(bf16[6144,128]{1,0:T(8,128)(2,1)} %refs_1_.5), channel_id=1, source_target_pairs={{0,2},{1,7},{2,0},{3,5},{4,6},{5,3},{6,4},{7,1},{8,10},{9,15},{10,... | collective-permute-start | bytes 4718600 | tf_op jit(solution)/shard_map/ppermute | solution.py:361
  26.5 1.4 copy-done
  27.9 1.4 copy-done.1
  29.3 1.3 shard_map.87
  30.5 1.9 %collective-permute-start.3 = (bf16[2,3072,128]{2,1,0:T(8,128)(2,1)}, bf16[2,3072,128]{2,1,0:T(8,128)(2,1)}, u32[]{:S(2)}, u32[]{:S(2)}) collective-permute-start(bf16[2,3072,128]{2,1,0:T(8,128)(2,1)} %shard_map.87), channel_id=1, source_target_pairs={{0,1},{1,0},{2,3},{3,2},{4,5},{5,4},{6,7},{7,6},{8,9},{9,8},{10,11... | collective-permute-start | bytes 4718600 | tf_op jit(solution)/shard_map/ppermute | solution.py:353
  32.4 5.3 %all-to-all-done.arrived_ref = bf16[16,4,768]{2,1,0:T(4,128)(2,1)S(1)} async-done(((bf16[16,4,768]{2,1,0:T(4,128)(2,1)}), bf16[16,4,768]{2,1,0:T(4,128)(2,1)S(1)}, u32[]{:S(2)}, u32[]{:S(2)}) %all-to-all-start) | async-done | bytes 98336 | tf_op jit(solution)/shard_map/all_to_all | solution.py:345
  37.7 1.9 %shard_map.86 = bf16[16,56,768]{2,1,0:T(8,128)(2,1)} custom-call(bf16[16,4,768]{2,1,0:T(4,128)(2,1)S(1)} %all-to-all-done.arrived_ref), custom_call_target="tpu_custom_call" | custom-call | tf_op jit(solution)/shard_map/pallas_call | solution.py:417
  39.6 6.0 %all-to-all-start.1 = ((bf16[16,56,768]{2,1,0:T(8,128)(2,1)}), bf16[16,56,768]{2,1,0:T(8,128)(2,1)S(1)}, u32[]{:S(2)}, u32[]{:S(2)}) async-start(bf16[16,56,768]{2,1,0:T(8,128)(2,1)} %shard_map.86), calls=%async_computation.1 | async-start | bytes 2752512 | tf_op jit(solution)/shard_map/all_to_all | solution.py:345
  47.1 2.0 %collective-permute-start.4 = (bf16[1,3072,128]{2,1,0:T(8,128)(2,1)}, bf16[1,3072,128]{2,1,0:T(8,128)(2,1)}, u32[]{:S(2)}, u32[]{:S(2)}) collective-permute-start(bf16[1,3072,128]{2,1,0:T(8,128)(2,1)} %shard_map.88), channel_id=1, source_target_pairs={{0,1},{1,0},{2,3},{3,2},{4,5},{5,4},{6,7},{7,6},{8,9},{9,8},{10,11... | collective-permute-start | bytes 2359304 | tf_op jit(solution)/shard_map/ppermute | solution.py:353
  49.1 1.2 shard_map.89
  50.3 2.4 %collective-permute-start.5 = (bf16[1,3072,128]{2,1,0:T(8,128)(2,1)S(1)}, bf16[1,3072,128]{2,1,0:T(8,128)(2,1)}, u32[]{:S(2)}, u32[]{:S(2)}) collective-permute-start(bf16[1,3072,128]{2,1,0:T(8,128)(2,1)S(1)} %shard_map.89), channel_id=1, source_target_pairs={{0,1},{1,0},{2,3},{3,2},{4,5},{5,4},{6,7},{7,6},{8,9},{9,8},{10,11... | collective-permute-start | bytes 2359304 | tf_op jit(solution)/shard_map/ppermute | solution.py:353
  53.1 4.1 %collective-permute-start = (bf16[192,128]{1,0:T(8,128)(2,1)S(1)}, bf16[192,128]{1,0:T(8,128)(2,1)S(1)}, u32[]{:S(2)}, u32[]{:S(2)}) collective-permute-start(bf16[192,128]{1,0:T(8,128)(2,1)S(1)} %bitcast.53), channel_id=1, source_target_pairs={{0,2},{1,7},{2,0},{3,5},{4,6},{5,3},{6,4},{7,1},{8,10},{9,15},{10,... | collective-permute-start | bytes 147464 | tf_op jit(solution)/shard_map/ppermute | solution.py:361
  57.3 8.2 %collective-permute-done.far_cot_ref = bf16[192,128]{1,0:T(8,128)(2,1)S(1)} collective-permute-done((bf16[192,128]{1,0:T(8,128)(2,1)S(1)}, bf16[192,128]{1,0:T(8,128)(2,1)S(1)}, u32[]{:S(2)}, u32[]{:S(2)}) %collective-permute-start) | collective-permute-done | bytes 49184 | tf_op jit(solution)/shard_map/ppermute | solution.py:361
  65.5 4.2 %shard_map.90 = (f32[192,512]{1,0:T(8,128)S(1)}, f32[192,512]{1,0:T(8,128)S(1)}) custom-call(s32[1]{0:T(128)} %bitcast.1.place_ref, bf16[16,56,768]{2,1,0:T(8,128)(2,1)S(1)} %all-to-all-done.1.rows_ref.refs_7_, bf16[6144,128]{1,0:T(8,128)(2,1)} %refs_0_.5, bf16[6144,128]{1,0:T(8,128)(2,1)} %refs_1_.5, bf16[6144,128]{1,0:T(8,128)(2,1)} %copy-done.2, ...), custom_call_target="tpu_custom_call" | custom-call | tf_op jit(solution)/shard_map/pallas_call | solution.py:436
  69.7 2.3 %collective-permute-start.6 = (f32[192,512]{1,0:T(8,128)S(1)}, f32[192,512]{1,0:T(8,128)S(1)}, u32[]{:S(2)}, u32[]{:S(2)}) collective-permute-start(f32[192,512]{1,0:T(8,128)S(1)} %get-tuple-element.28), channel_id=1, source_target_pairs={{0,1},{1,0},{2,3},{3,2},{4,5},{5,4},{6,7},{7,6},{8,9},{9,8},{10,11... | collective-permute-start | bytes 1179656 | tf_op jit(solution)/shard_map/ppermute | solution.py:353
  72.0 1.3 collective-permute-done.6.core_ref
  73.7 2.3 %collective-permute-start.7 = (bf16[192,640]{1,0:T(8,128)(2,1)S(1)}, bf16[192,640]{1,0:T(8,128)(2,1)S(1)}, u32[]{:S(2)}, u32[]{:S(2)}) collective-permute-start(bf16[192,640]{1,0:T(8,128)(2,1)S(1)} %get-tuple-element.32.own_ref), channel_id=1, source_target_pairs={{0,1},{1,0},{2,3},{3,2},{4,5},{5,4},{6,7},{7,6},{8,9},{9,8},{10,11... | collective-permute-start | bytes 737288 | tf_op jit(solution)/shard_map/ppermute | solution.py:353
  76.0 1.1 collective-permute-done.7.core_ref
  77.1 6.6 %shard_map.92 = bf16[16,56,768]{2,1,0:T(8,128)(2,1)} custom-call(s32[1]{0:T(128)} %bitcast.1.place_ref, bf16[192,640]{1,0:T(8,128)(2,1)S(1)} %get-tuple-element.32.own_ref, bf16[192,640]{1,0:T(8,128)(2,1)S(1)} %collective-permute-done.7.core_ref, f32[192,128]{1,0:T(8,128)S(1)} %get-tuple-element.33.coef_ref, bf16[6144,128]{1,0:T(8,128)(2,1)} %refs_0_.5, ...), custom_call_target="tpu_custom_call" | custom-call | tf_op jit(solution)/shard_map/pallas_call | solution.py:455
  83.8 7.0 %all-to-all-start.2 = ((bf16[16,56,768]{2,1,0:T(8,128)(2,1)}), bf16[16,56,768]{2,1,0:T(8,128)(2,1)S(1)}, u32[]{:S(2)}, u32[]{:S(2)}) async-start(bf16[16,56,768]{2,1,0:T(8,128)(2,1)} %shard_map.92), calls=%async_computation.2 | async-start | bytes 2752512 | tf_op jit(solution)/shard_map/all_to_all | solution.py:345
  91.8 3.6 %collective-permute-start.8 = (bf16[192,128]{1,0:T(8,128)(2,1)S(1)}, bf16[192,128]{1,0:T(8,128)(2,1)S(1)}, u32[]{:S(2)}, u32[]{:S(2)}) collective-permute-start(bf16[192,128]{1,0:T(8,128)(2,1)S(1)} %get-tuple-element.34), channel_id=1, source_target_pairs={{0,2},{1,7},{2,0},{3,5},{4,6},{5,3},{6,4},{7,1},{8,10},{9,15},{10,... | collective-permute-start | bytes 147464 | tf_op jit(solution)/shard_map/ppermute | solution.py:361
  96.3 13.1 %all-to-all-done.2.recv_ref = bf16[16,56,768]{2,1,0:T(8,128)(2,1)S(1)} async-done(((bf16[16,56,768]{2,1,0:T(8,128)(2,1)}), bf16[16,56,768]{2,1,0:T(8,128)(2,1)S(1)}, u32[]{:S(2)}, u32[]{:S(2)}) %all-to-all-start.2) | async-done | bytes 1376288 | tf_op jit(solution)/shard_map/all_to_all | solution.py:345
  109.4 1.2 shard_map.93
  110.6 13.1 %all-to-all-start.3 = ((bf16[16,8,512]{2,1,0:T(8,128)(2,1)}), bf16[16,8,512]{2,1,0:T(8,128)(2,1)S(1)}, u32[]{:S(2)}, u32[]{:S(2)}) async-start(bf16[16,8,512]{2,1,0:T(8,128)(2,1)} %bitcast.14), calls=%async_computation.3 | async-start | bytes 262144 | tf_op jit(solution)/shard_map/all_to_all | solution.py:345
  124.4 15.3 %all-to-all-done.3.home_ref = bf16[16,8,512]{2,1,0:T(8,128)(2,1)S(1)} async-done(((bf16[16,8,512]{2,1,0:T(8,128)(2,1)}), bf16[16,8,512]{2,1,0:T(8,128)(2,1)S(1)}, u32[]{:S(2)}, u32[]{:S(2)}) %all-to-all-start.3) | async-done | bytes 131104 | tf_op jit(solution)/shard_map/all_to_all | solution.py:345
  140.9 4.7 %all-to-all-start.4 = ((f32[16,2,768]{2,1,0:T(2,128)}), f32[16,2,768]{2,1,0:T(2,128)S(1)}, u32[]{:S(2)}, u32[]{:S(2)}) async-start(f32[16,2,768]{2,1,0:T(2,128)} %shard_map.94), calls=%async_computation.4 | async-start | bytes 196608 | tf_op jit(solution)/shard_map/all_to_all | solution.py:345
  146.3 5.3 %all-to-all-done.4.router_ref = f32[16,2,768]{2,1,0:T(2,128)S(1)} async-done(((f32[16,2,768]{2,1,0:T(2,128)}), f32[16,2,768]{2,1,0:T(2,128)S(1)}, u32[]{:S(2)}, u32[]{:S(2)}) %all-to-all-start.4) | async-done | bytes 98336 | tf_op jit(solution)/shard_map/all_to_all | solution.py:345
  152.4 3.5 %all-to-all-start.5 = ((bf16[4,24,1536]{2,1,0:T(8,128)(2,1)}), bf16[4,24,1536]{2,1,0:T(8,128)(2,1)S(1)}, u32[]{:S(2)}, u32[]{:S(2)}) async-start(bf16[4,24,1536]{2,1,0:T(8,128)(2,1)} %shard_map.95), calls=%async_computation.5 | async-start | bytes 589824 | tf_op jit(solution)/shard_map/all_to_all | solution.py:345
  156.6 5.5 %all-to-all-done.5.got_ref = bf16[4,24,1536]{2,1,0:T(8,128)(2,1)S(1)} async-done(((bf16[4,24,1536]{2,1,0:T(8,128)(2,1)}), bf16[4,24,1536]{2,1,0:T(8,128)(2,1)S(1)}, u32[]{:S(2)}, u32[]{:S(2)}) %all-to-all-start.5) | async-done | bytes 294944 | tf_op jit(solution)/shard_map/all_to_all | solution.py:345
  (75 shorter events, 8.6 us)
Async XLA Ops:
  0.6 45.0 %collective-permute-start.1 = (bf16[6144,128]{1,0:T(8,128)(2,1)}, bf16[6144,128]{1,0:T(8,128)(2,1)S(1)}, u32[]{:S(2)}, u32[]{:S(2)}) collective-permute-start(bf16[6144,128]{1,0:T(8,128)(2,1)} %refs_0_.5), channel_id=1, source_target_pairs={{0,2},{1,7},{2,0},{3,5},{4,6},{5,3},{6,4},{7,1},{8,10},{9,15},{10,... | collective-permute-start | bytes 4718600 | tf_op jit(solution)/shard_map/ppermute | solution.py:361
  7.9 29.8 %all-to-all-start = ((bf16[16,4,768]{2,1,0:T(4,128)(2,1)}), bf16[16,4,768]{2,1,0:T(4,128)(2,1)S(1)}, u32[]{:S(2)}, u32[]{:S(2)}) async-start(bf16[16,4,768]{2,1,0:T(4,128)(2,1)} %bitcast.52), calls=%async_computation | async-start | bytes 196608 | tf_op jit(solution)/shard_map/all_to_all | solution.py:345
  23.2 26.0 %collective-permute-start.2 = (bf16[6144,128]{1,0:T(8,128)(2,1)}, bf16[6144,128]{1,0:T(8,128)(2,1)}, u32[]{:S(2)}, u32[]{:S(2)}) collective-permute-start(bf16[6144,128]{1,0:T(8,128)(2,1)} %refs_1_.5), channel_id=1, source_target_pairs={{0,2},{1,7},{2,0},{3,5},{4,6},{5,3},{6,4},{7,1},{8,10},{9,15},{10,... | collective-permute-start | bytes 4718600 | tf_op jit(solution)/shard_map/ppermute | solution.py:361
  26.5 1.4 copy-start
  27.9 1.4 copy-start.1
  30.5 35.0 %collective-permute-start.3 = (bf16[2,3072,128]{2,1,0:T(8,128)(2,1)}, bf16[2,3072,128]{2,1,0:T(8,128)(2,1)}, u32[]{:S(2)}, u32[]{:S(2)}) collective-permute-start(bf16[2,3072,128]{2,1,0:T(8,128)(2,1)} %shard_map.87), channel_id=1, source_target_pairs={{0,1},{1,0},{2,3},{3,2},{4,5},{5,4},{6,7},{7,6},{8,9},{9,8},{10,11... | collective-permute-start | bytes 4718600 | tf_op jit(solution)/shard_map/ppermute | solution.py:353
  39.6 25.9 %all-to-all-start.1 = ((bf16[16,56,768]{2,1,0:T(8,128)(2,1)}), bf16[16,56,768]{2,1,0:T(8,128)(2,1)S(1)}, u32[]{:S(2)}, u32[]{:S(2)}) async-start(bf16[16,56,768]{2,1,0:T(8,128)(2,1)} %shard_map.86), calls=%async_computation.1 | async-start | bytes 2752512 | tf_op jit(solution)/shard_map/all_to_all | solution.py:345
  45.7 1.4 copy-start.2
  47.1 5.7 %copy-start.3 = (bf16[384,128]{1,0:T(8,128)(2,1)S(1)}, bf16[384,128]{1,0:T(8,128)(2,1)}, u32[]{:S(2)}) copy-start(bf16[384,128]{1,0:T(8,128)(2,1)} %param.11) | copy-start | bytes 294916
  47.1 18.4 %collective-permute-start.4 = (bf16[1,3072,128]{2,1,0:T(8,128)(2,1)}, bf16[1,3072,128]{2,1,0:T(8,128)(2,1)}, u32[]{:S(2)}, u32[]{:S(2)}) collective-permute-start(bf16[1,3072,128]{2,1,0:T(8,128)(2,1)} %shard_map.88), channel_id=1, source_target_pairs={{0,1},{1,0},{2,3},{3,2},{4,5},{5,4},{6,7},{7,6},{8,9},{9,8},{10,11... | collective-permute-start | bytes 2359304 | tf_op jit(solution)/shard_map/ppermute | solution.py:353
  50.3 15.2 %collective-permute-start.5 = (bf16[1,3072,128]{2,1,0:T(8,128)(2,1)S(1)}, bf16[1,3072,128]{2,1,0:T(8,128)(2,1)}, u32[]{:S(2)}, u32[]{:S(2)}) collective-permute-start(bf16[1,3072,128]{2,1,0:T(8,128)(2,1)S(1)} %shard_map.89), channel_id=1, source_target_pairs={{0,1},{1,0},{2,3},{3,2},{4,5},{5,4},{6,7},{7,6},{8,9},{9,8},{10,11... | collective-permute-start | bytes 2359304 | tf_op jit(solution)/shard_map/ppermute | solution.py:353
  53.1 12.3 %collective-permute-start = (bf16[192,128]{1,0:T(8,128)(2,1)S(1)}, bf16[192,128]{1,0:T(8,128)(2,1)S(1)}, u32[]{:S(2)}, u32[]{:S(2)}) collective-permute-start(bf16[192,128]{1,0:T(8,128)(2,1)S(1)} %bitcast.53), channel_id=1, source_target_pairs={{0,2},{1,7},{2,0},{3,5},{4,6},{5,3},{6,4},{7,1},{8,10},{9,15},{10,... | collective-permute-start | bytes 147464 | tf_op jit(solution)/shard_map/ppermute | solution.py:361
  69.7 3.6 %collective-permute-start.6 = (f32[192,512]{1,0:T(8,128)S(1)}, f32[192,512]{1,0:T(8,128)S(1)}, u32[]{:S(2)}, u32[]{:S(2)}) collective-permute-start(f32[192,512]{1,0:T(8,128)S(1)} %get-tuple-element.28), channel_id=1, source_target_pairs={{0,1},{1,0},{2,3},{3,2},{4,5},{5,4},{6,7},{7,6},{8,9},{9,8},{10,11... | collective-permute-start | bytes 1179656 | tf_op jit(solution)/shard_map/ppermute | solution.py:353
  73.7 3.4 %collective-permute-start.7 = (bf16[192,640]{1,0:T(8,128)(2,1)S(1)}, bf16[192,640]{1,0:T(8,128)(2,1)S(1)}, u32[]{:S(2)}, u32[]{:S(2)}) collective-permute-start(bf16[192,640]{1,0:T(8,128)(2,1)S(1)} %get-tuple-element.32.own_ref), channel_id=1, source_target_pairs={{0,1},{1,0},{2,3},{3,2},{4,5},{5,4},{6,7},{7,6},{8,9},{9,8},{10,11... | collective-permute-start | bytes 737288 | tf_op jit(solution)/shard_map/ppermute | solution.py:353
  83.7 7.0 %copy-start.4 = (s32[8,2]{0,1:T(2,128)S(1)}, s32[8,2]{0,1:T(2,128)}, u32[]{:S(2)}) copy-start(s32[8,2]{0,1:T(2,128)} %param.7) | copy-start | bytes 196
  83.7 7.6 %copy-start.5 = (f32[8,8]{1,0:T(8,128)S(1)}, f32[8,8]{1,0:T(8,128)}, u32[]{:S(2)}) copy-start(f32[8,8]{1,0:T(8,128)} %get-tuple-element.35) | copy-start | bytes 772
  83.8 25.7 %all-to-all-start.2 = ((bf16[16,56,768]{2,1,0:T(8,128)(2,1)}), bf16[16,56,768]{2,1,0:T(8,128)(2,1)S(1)}, u32[]{:S(2)}, u32[]{:S(2)}) async-start(bf16[16,56,768]{2,1,0:T(8,128)(2,1)} %shard_map.92), calls=%async_computation.2 | async-start | bytes 2752512 | tf_op jit(solution)/shard_map/all_to_all | solution.py:345
  91.8 18.9 %collective-permute-start.8 = (bf16[192,128]{1,0:T(8,128)(2,1)S(1)}, bf16[192,128]{1,0:T(8,128)(2,1)S(1)}, u32[]{:S(2)}, u32[]{:S(2)}) collective-permute-start(bf16[192,128]{1,0:T(8,128)(2,1)S(1)} %get-tuple-element.34), channel_id=1, source_target_pairs={{0,2},{1,7},{2,0},{3,5},{4,6},{5,3},{6,4},{7,1},{8,10},{9,15},{10,... | collective-permute-start | bytes 147464 | tf_op jit(solution)/shard_map/ppermute | solution.py:361
  110.6 29.0 %all-to-all-start.3 = ((bf16[16,8,512]{2,1,0:T(8,128)(2,1)}), bf16[16,8,512]{2,1,0:T(8,128)(2,1)S(1)}, u32[]{:S(2)}, u32[]{:S(2)}) async-start(bf16[16,8,512]{2,1,0:T(8,128)(2,1)} %bitcast.14), calls=%async_computation.3 | async-start | bytes 262144 | tf_op jit(solution)/shard_map/all_to_all | solution.py:345
  140.9 10.6 %all-to-all-start.4 = ((f32[16,2,768]{2,1,0:T(2,128)}), f32[16,2,768]{2,1,0:T(2,128)S(1)}, u32[]{:S(2)}, u32[]{:S(2)}) async-start(f32[16,2,768]{2,1,0:T(2,128)} %shard_map.94), calls=%async_computation.4 | async-start | bytes 196608 | tf_op jit(solution)/shard_map/all_to_all | solution.py:345
  152.4 9.8 %all-to-all-start.5 = ((bf16[4,24,1536]{2,1,0:T(8,128)(2,1)}), bf16[4,24,1536]{2,1,0:T(8,128)(2,1)S(1)}, u32[]{:S(2)}, u32[]{:S(2)}) async-start(bf16[4,24,1536]{2,1,0:T(8,128)(2,1)} %shard_map.95), calls=%async_computation.5 | async-start | bytes 589824 | tf_op jit(solution)/shard_map/all_to_all | solution.py:345

commit v4 on v3

--- a/solution.py
+++ b/solution.py
@@ -103,7 +103,7 @@
         notes = jnp.concatenate([jnp.concatenate(rows, axis=0), rest], axis=1)
         block_ref[GROUP:BLOCK, :] = notes.astype(bf16)
 
-    for i in range(M):
+    for i in range(Y * M):
         out_ref[i] = block_ref[...]
 
 
@@ -416,9 +416,9 @@
     rows_spec = pl.BlockSpec((M, BLOCK, piece), lambda i: (i, 0, 0))
     gathered = call(
         gather_kernel,
-        (Y,),
+        (1,),
         [whole(E * C, MOST + 1, piece)],
-        rows_spec,
+        whole(Y * M, BLOCK, piece),
         HBM((Y * M, BLOCK, piece), bf16),
         [pltpu.VMEM((BLOCK, piece), bf16)],
     )(arrived)

time: 164 us -> 164 us (level)
  no operation moved by 1% of the time
where the time goes in v4:
time: 164 us; the launch traced here: 163 us
  starting transfers between devices  77.4 us (47%)
  waiting for transfers between devices  55.2 us (34%)
  Pallas kernels  21.5 us (13%)
  local copies, waits for them, and re-layouts  4.92 us (3%)
  other arithmetic  2.4 us (1%)
    all_to_all x6, starting transfers between devices, a2a(): return lax.all_to_all(v, axes, split_axis=0, concat_axis=0, tiled=True)  50.1 us
    all_to_all x6, waiting for transfers between devices, a2a(): return lax.all_to_all(v, axes, split_axis=0, concat_axis=0, tiled=True)  44.6 us
    ppermute x4, starting transfers between devices, along_x(): return lax.ppermute(v, ('xh', 'xl', 'core'), order)  16.3 us
    ppermute x5, starting transfers between devices, swap(): return lax.ppermute(v, 'core', [(0, 1), (1, 0)])  10.9 us
    ppermute x4, waiting for transfers between devices, along_x(): return lax.ppermute(v, ('xh', 'xl', 'core'), order)  8.16 us
    pallas_call x1, Pallas kernels, local(): placed(dx_kernel, (Y,), [whole(slots, 640)] * 2 + [whole(slots, 128)] + w...  6.63 us
    pallas_call x1, Pallas kernels, local(): placed(pre_kernel, (1,), [whole(Y * M, BLOCK, piece)] + w_specs(half, 1),...  4.18 us
    pallas_call x3, Pallas kernels, other_half(): pl.pallas_call(half_kernel, grid_spec=pltpu.PrefetchScalarGridSpec(num_sc...  3.47 us
  transfers between devices with their start and end apart: 15, of which 8 were waited for; matrix products, arithmetic and copies ran while one was open for 2% of the time, Pallas kernels for 5%

profile of v4, /device:TPU:1, one launch (start us, length us, event | category | flops | bytes accessed | tf_op | source)
XLA Modules:
  0.0 162.9 jit_solution(7117219175514412328)
XLA Ops:
  0.6 5.2 %collective-permute-start.1 = (bf16[6144,128]{1,0:T(8,128)(2,1)}, bf16[6144,128]{1,0:T(8,128)(2,1)S(1)}, u32[]{:S(2)}, u32[]{:S(2)}) collective-permute-start(bf16[6144,128]{1,0:T(8,128)(2,1)} %refs_0_.5), channel_id=1, source_target_pairs={{0,2},{1,7},{2,0},{3,5},{4,6},{5,3},{6,4},{7,1},{8,10},{9,15},{10,... | collective-permute-start | bytes 4718600 | tf_op jit(solution)/shard_map/ppermute | solution.py:361
  5.9 2.1 %shard_map.85 = (bf16[8,2,4,768]{3,2,1,0:T(4,128)(2,1)}, f32[8,8]{1,0:T(8,128)}) custom-call(s32[1]{0:T(128)} %bitcast.2.place_ref, s32[2,8]{1,0:T(2,128)} %bitcast.54, bf16[8,6144]{1,0:T(8,128)(2,1)} %tokens_ref.1, bf16[8,6144]{1,0:T(8,128)(2,1)} %bitcast.50), custom_call_target="tpu_custom_call" | custom-call | tf_op jit(solution)/shard_map/pallas_call | solution.py:379
  7.9 15.2 %all-to-all-start = ((bf16[16,4,768]{2,1,0:T(4,128)(2,1)}), bf16[16,4,768]{2,1,0:T(4,128)(2,1)S(1)}, u32[]{:S(2)}, u32[]{:S(2)}) async-start(bf16[16,4,768]{2,1,0:T(4,128)(2,1)} %bitcast.52), calls=%async_computation | async-start | bytes 196608 | tf_op jit(solution)/shard_map/all_to_all | solution.py:345
  23.2 3.3 %collective-permute-start.2 = (bf16[6144,128]{1,0:T(8,128)(2,1)}, bf16[6144,128]{1,0:T(8,128)(2,1)}, u32[]{:S(2)}, u32[]{:S(2)}) collective-permute-start(bf16[6144,128]{1,0:T(8,128)(2,1)} %refs_1_.5), channel_id=1, source_target_pairs={{0,2},{1,7},{2,0},{3,5},{4,6},{5,3},{6,4},{7,1},{8,10},{9,15},{10,... | collective-permute-start | bytes 4718600 | tf_op jit(solution)/shard_map/ppermute | solution.py:361
  26.5 1.4 copy-done
  27.9 1.4 copy-done.1
  29.3 1.3 shard_map.87
  30.5 1.9 %collective-permute-start.3 = (bf16[2,3072,128]{2,1,0:T(8,128)(2,1)}, bf16[2,3072,128]{2,1,0:T(8,128)(2,1)}, u32[]{:S(2)}, u32[]{:S(2)}) collective-permute-start(bf16[2,3072,128]{2,1,0:T(8,128)(2,1)} %shard_map.87), channel_id=1, source_target_pairs={{0,1},{1,0},{2,3},{3,2},{4,5},{5,4},{6,7},{7,6},{8,9},{9,8},{10,11... | collective-permute-start | bytes 4718600 | tf_op jit(solution)/shard_map/ppermute | solution.py:353
  32.4 5.3 %all-to-all-done.arrived_ref = bf16[16,4,768]{2,1,0:T(4,128)(2,1)S(1)} async-done(((bf16[16,4,768]{2,1,0:T(4,128)(2,1)}), bf16[16,4,768]{2,1,0:T(4,128)(2,1)S(1)}, u32[]{:S(2)}, u32[]{:S(2)}) %all-to-all-start) | async-done | bytes 98336 | tf_op jit(solution)/shard_map/all_to_all | solution.py:345
  37.7 1.3 shard_map.86
  39.1 6.0 %all-to-all-start.1 = ((bf16[16,56,768]{2,1,0:T(8,128)(2,1)}), bf16[16,56,768]{2,1,0:T(8,128)(2,1)S(1)}, u32[]{:S(2)}, u32[]{:S(2)}) async-start(bf16[16,56,768]{2,1,0:T(8,128)(2,1)} %shard_map.86), calls=%async_computation.1 | async-start | bytes 2752512 | tf_op jit(solution)/shard_map/all_to_all | solution.py:345
  46.5 2.0 %collective-permute-start.4 = (bf16[1,3072,128]{2,1,0:T(8,128)(2,1)}, bf16[1,3072,128]{2,1,0:T(8,128)(2,1)}, u32[]{:S(2)}, u32[]{:S(2)}) collective-permute-start(bf16[1,3072,128]{2,1,0:T(8,128)(2,1)} %shard_map.88), channel_id=1, source_target_pairs={{0,1},{1,0},{2,3},{3,2},{4,5},{5,4},{6,7},{7,6},{8,9},{9,8},{10,11... | collective-permute-start | bytes 2359304 | tf_op jit(solution)/shard_map/ppermute | solution.py:353
  48.6 1.2 shard_map.89
  49.8 2.4 %collective-permute-start.5 = (bf16[1,3072,128]{2,1,0:T(8,128)(2,1)S(1)}, bf16[1,3072,128]{2,1,0:T(8,128)(2,1)}, u32[]{:S(2)}, u32[]{:S(2)}) collective-permute-start(bf16[1,3072,128]{2,1,0:T(8,128)(2,1)S(1)} %shard_map.89), channel_id=1, source_target_pairs={{0,1},{1,0},{2,3},{3,2},{4,5},{5,4},{6,7},{7,6},{8,9},{9,8},{10,11... | collective-permute-start | bytes 2359304 | tf_op jit(solution)/shard_map/ppermute | solution.py:353
  52.6 4.1 %collective-permute-start = (bf16[192,128]{1,0:T(8,128)(2,1)S(1)}, bf16[192,128]{1,0:T(8,128)(2,1)S(1)}, u32[]{:S(2)}, u32[]{:S(2)}) collective-permute-start(bf16[192,128]{1,0:T(8,128)(2,1)S(1)} %bitcast.53), channel_id=1, source_target_pairs={{0,2},{1,7},{2,0},{3,5},{4,6},{5,3},{6,4},{7,1},{8,10},{9,15},{10,... | collective-permute-start | bytes 147464 | tf_op jit(solution)/shard_map/ppermute | solution.py:361
  56.8 8.2 %collective-permute-done.far_cot_ref = bf16[192,128]{1,0:T(8,128)(2,1)S(1)} collective-permute-done((bf16[192,128]{1,0:T(8,128)(2,1)S(1)}, bf16[192,128]{1,0:T(8,128)(2,1)S(1)}, u32[]{:S(2)}, u32[]{:S(2)}) %collective-permute-start) | collective-permute-done | bytes 49184 | tf_op jit(solution)/shard_map/ppermute | solution.py:361
  65.0 4.2 %shard_map.90 = (f32[192,512]{1,0:T(8,128)S(1)}, f32[192,512]{1,0:T(8,128)S(1)}) custom-call(s32[1]{0:T(128)} %bitcast.1.place_ref, bf16[16,56,768]{2,1,0:T(8,128)(2,1)S(1)} %all-to-all-done.1.rows_ref.refs_7_, bf16[6144,128]{1,0:T(8,128)(2,1)} %refs_0_.5, bf16[6144,128]{1,0:T(8,128)(2,1)} %refs_1_.5, bf16[6144,128]{1,0:T(8,128)(2,1)} %copy-done.2, ...), custom_call_target="tpu_custom_call" | custom-call | tf_op jit(solution)/shard_map/pallas_call | solution.py:436
  69.1 2.3 %collective-permute-start.6 = (f32[192,512]{1,0:T(8,128)S(1)}, f32[192,512]{1,0:T(8,128)S(1)}, u32[]{:S(2)}, u32[]{:S(2)}) collective-permute-start(f32[192,512]{1,0:T(8,128)S(1)} %get-tuple-element.28), channel_id=1, source_target_pairs={{0,1},{1,0},{2,3},{3,2},{4,5},{5,4},{6,7},{7,6},{8,9},{9,8},{10,11... | collective-permute-start | bytes 1179656 | tf_op jit(solution)/shard_map/ppermute | solution.py:353
  71.5 1.3 collective-permute-done.6.core_ref
  73.2 2.3 %collective-permute-start.7 = (bf16[192,640]{1,0:T(8,128)(2,1)S(1)}, bf16[192,640]{1,0:T(8,128)(2,1)S(1)}, u32[]{:S(2)}, u32[]{:S(2)}) collective-permute-start(bf16[192,640]{1,0:T(8,128)(2,1)S(1)} %get-tuple-element.32.own_ref), channel_id=1, source_target_pairs={{0,1},{1,0},{2,3},{3,2},{4,5},{5,4},{6,7},{7,6},{8,9},{9,8},{10,11... | collective-permute-start | bytes 737288 | tf_op jit(solution)/shard_map/ppermute | solution.py:353
  75.5 1.1 collective-permute-done.7.core_ref
  76.6 6.6 %shard_map.92 = bf16[16,56,768]{2,1,0:T(8,128)(2,1)} custom-call(s32[1]{0:T(128)} %bitcast.1.place_ref, bf16[192,640]{1,0:T(8,128)(2,1)S(1)} %get-tuple-element.32.own_ref, bf16[192,640]{1,0:T(8,128)(2,1)S(1)} %collective-permute-done.7.core_ref, f32[192,128]{1,0:T(8,128)S(1)} %get-tuple-element.33.coef_ref, bf16[6144,128]{1,0:T(8,128)(2,1)} %refs_0_.5, ...), custom_call_target="tpu_custom_call" | custom-call | tf_op jit(solution)/shard_map/pallas_call | solution.py:455
  83.2 7.0 %all-to-all-start.2 = ((bf16[16,56,768]{2,1,0:T(8,128)(2,1)}), bf16[16,56,768]{2,1,0:T(8,128)(2,1)S(1)}, u32[]{:S(2)}, u32[]{:S(2)}) async-start(bf16[16,56,768]{2,1,0:T(8,128)(2,1)} %shard_map.92), calls=%async_computation.2 | async-start | bytes 2752512 | tf_op jit(solution)/shard_map/all_to_all | solution.py:345
  91.2 3.6 %collective-permute-start.8 = (bf16[192,128]{1,0:T(8,128)(2,1)S(1)}, bf16[192,128]{1,0:T(8,128)(2,1)S(1)}, u32[]{:S(2)}, u32[]{:S(2)}) collective-permute-start(bf16[192,128]{1,0:T(8,128)(2,1)S(1)} %get-tuple-element.34), channel_id=1, source_target_pairs={{0,2},{1,7},{2,0},{3,5},{4,6},{5,3},{6,4},{7,1},{8,10},{9,15},{10,... | collective-permute-start | bytes 147464 | tf_op jit(solution)/shard_map/ppermute | solution.py:361
  95.7 13.1 %all-to-all-done.2.recv_ref = bf16[16,56,768]{2,1,0:T(8,128)(2,1)S(1)} async-done(((bf16[16,56,768]{2,1,0:T(8,128)(2,1)}), bf16[16,56,768]{2,1,0:T(8,128)(2,1)S(1)}, u32[]{:S(2)}, u32[]{:S(2)}) %all-to-all-start.2) | async-done | bytes 1376288 | tf_op jit(solution)/shard_map/all_to_all | solution.py:345
  108.9 1.2 shard_map.93
  110.1 13.7 %all-to-all-start.3 = ((bf16[16,8,512]{2,1,0:T(8,128)(2,1)}), bf16[16,8,512]{2,1,0:T(8,128)(2,1)S(1)}, u32[]{:S(2)}, u32[]{:S(2)}) async-start(bf16[16,8,512]{2,1,0:T(8,128)(2,1)} %bitcast.14), calls=%async_computation.3 | async-start | bytes 262144 | tf_op jit(solution)/shard_map/all_to_all | solution.py:345
  124.4 15.3 %all-to-all-done.3.home_ref = bf16[16,8,512]{2,1,0:T(8,128)(2,1)S(1)} async-done(((bf16[16,8,512]{2,1,0:T(8,128)(2,1)}), bf16[16,8,512]{2,1,0:T(8,128)(2,1)S(1)}, u32[]{:S(2)}, u32[]{:S(2)}) %all-to-all-start.3) | async-done | bytes 131104 | tf_op jit(solution)/shard_map/all_to_all | solution.py:345
  140.9 4.7 %all-to-all-start.4 = ((f32[16,2,768]{2,1,0:T(2,128)}), f32[16,2,768]{2,1,0:T(2,128)S(1)}, u32[]{:S(2)}, u32[]{:S(2)}) async-start(f32[16,2,768]{2,1,0:T(2,128)} %shard_map.94), calls=%async_computation.4 | async-start | bytes 196608 | tf_op jit(solution)/shard_map/all_to_all | solution.py:345
  146.3 5.3 %all-to-all-done.4.router_ref = f32[16,2,768]{2,1,0:T(2,128)S(1)} async-done(((f32[16,2,768]{2,1,0:T(2,128)}), f32[16,2,768]{2,1,0:T(2,128)S(1)}, u32[]{:S(2)}, u32[]{:S(2)}) %all-to-all-start.4) | async-done | bytes 98336 | tf_op jit(solution)/shard_map/all_to_all | solution.py:345
  152.4 3.5 %all-to-all-start.5 = ((bf16[4,24,1536]{2,1,0:T(8,128)(2,1)}), bf16[4,24,1536]{2,1,0:T(8,128)(2,1)S(1)}, u32[]{:S(2)}, u32[]{:S(2)}) async-start(bf16[4,24,1536]{2,1,0:T(8,128)(2,1)} %shard_map.95), calls=%async_computation.5 | async-start | bytes 589824 | tf_op jit(solution)/shard_map/all_to_all | solution.py:345
  156.6 5.5 %all-to-all-done.5.got_ref = bf16[4,24,1536]{2,1,0:T(8,128)(2,1)S(1)} async-done(((bf16[4,24,1536]{2,1,0:T(8,128)(2,1)}), bf16[4,24,1536]{2,1,0:T(8,128)(2,1)S(1)}, u32[]{:S(2)}, u32[]{:S(2)}) %all-to-all-start.5) | async-done | bytes 294944 | tf_op jit(solution)/shard_map/all_to_all | solution.py:345
  (75 shorter events, 8.6 us)
Async XLA Ops:
  0.6 44.5 %collective-permute-start.1 = (bf16[6144,128]{1,0:T(8,128)(2,1)}, bf16[6144,128]{1,0:T(8,128)(2,1)S(1)}, u32[]{:S(2)}, u32[]{:S(2)}) collective-permute-start(bf16[6144,128]{1,0:T(8,128)(2,1)} %refs_0_.5), channel_id=1, source_target_pairs={{0,2},{1,7},{2,0},{3,5},{4,6},{5,3},{6,4},{7,1},{8,10},{9,15},{10,... | collective-permute-start | bytes 4718600 | tf_op jit(solution)/shard_map/ppermute | solution.py:361
  7.9 29.8 %all-to-all-start = ((bf16[16,4,768]{2,1,0:T(4,128)(2,1)}), bf16[16,4,768]{2,1,0:T(4,128)(2,1)S(1)}, u32[]{:S(2)}, u32[]{:S(2)}) async-start(bf16[16,4,768]{2,1,0:T(4,128)(2,1)} %bitcast.52), calls=%async_computation | async-start | bytes 196608 | tf_op jit(solution)/shard_map/all_to_all | solution.py:345
  23.2 25.4 %collective-permute-start.2 = (bf16[6144,128]{1,0:T(8,128)(2,1)}, bf16[6144,128]{1,0:T(8,128)(2,1)}, u32[]{:S(2)}, u32[]{:S(2)}) collective-permute-start(bf16[6144,128]{1,0:T(8,128)(2,1)} %refs_1_.5), channel_id=1, source_target_pairs={{0,2},{1,7},{2,0},{3,5},{4,6},{5,3},{6,4},{7,1},{8,10},{9,15},{10,... | collective-permute-start | bytes 4718600 | tf_op jit(solution)/shard_map/ppermute | solution.py:361
  26.5 1.4 copy-start
  27.9 1.4 copy-start.1
  30.5 34.4 %collective-permute-start.3 = (bf16[2,3072,128]{2,1,0:T(8,128)(2,1)}, bf16[2,3072,128]{2,1,0:T(8,128)(2,1)}, u32[]{:S(2)}, u32[]{:S(2)}) collective-permute-start(bf16[2,3072,128]{2,1,0:T(8,128)(2,1)} %shard_map.87), channel_id=1, source_target_pairs={{0,1},{1,0},{2,3},{3,2},{4,5},{5,4},{6,7},{7,6},{8,9},{9,8},{10,11... | collective-permute-start | bytes 4718600 | tf_op jit(solution)/shard_map/ppermute | solution.py:353
  39.1 25.9 %all-to-all-start.1 = ((bf16[16,56,768]{2,1,0:T(8,128)(2,1)}), bf16[16,56,768]{2,1,0:T(8,128)(2,1)S(1)}, u32[]{:S(2)}, u32[]{:S(2)}) async-start(bf16[16,56,768]{2,1,0:T(8,128)(2,1)} %shard_map.86), calls=%async_computation.1 | async-start | bytes 2752512 | tf_op jit(solution)/shard_map/all_to_all | solution.py:345
  45.1 1.4 copy-start.2
  46.5 5.7 %copy-start.3 = (bf16[384,128]{1,0:T(8,128)(2,1)S(1)}, bf16[384,128]{1,0:T(8,128)(2,1)}, u32[]{:S(2)}) copy-start(bf16[384,128]{1,0:T(8,128)(2,1)} %param.11) | copy-start | bytes 294916
  46.5 18.4 %collective-permute-start.4 = (bf16[1,3072,128]{2,1,0:T(8,128)(2,1)}, bf16[1,3072,128]{2,1,0:T(8,128)(2,1)}, u32[]{:S(2)}, u32[]{:S(2)}) collective-permute-start(bf16[1,3072,128]{2,1,0:T(8,128)(2,1)} %shard_map.88), channel_id=1, source_target_pairs={{0,1},{1,0},{2,3},{3,2},{4,5},{5,4},{6,7},{7,6},{8,9},{9,8},{10,11... | collective-permute-start | bytes 2359304 | tf_op jit(solution)/shard_map/ppermute | solution.py:353
  49.8 15.2 %collective-permute-start.5 = (bf16[1,3072,128]{2,1,0:T(8,128)(2,1)S(1)}, bf16[1,3072,128]{2,1,0:T(8,128)(2,1)}, u32[]{:S(2)}, u32[]{:S(2)}) collective-permute-start(bf16[1,3072,128]{2,1,0:T(8,128)(2,1)S(1)} %shard_map.89), channel_id=1, source_target_pairs={{0,1},{1,0},{2,3},{3,2},{4,5},{5,4},{6,7},{7,6},{8,9},{9,8},{10,11... | collective-permute-start | bytes 2359304 | tf_op jit(solution)/shard_map/ppermute | solution.py:353
  52.6 12.3 %collective-permute-start = (bf16[192,128]{1,0:T(8,128)(2,1)S(1)}, bf16[192,128]{1,0:T(8,128)(2,1)S(1)}, u32[]{:S(2)}, u32[]{:S(2)}) collective-permute-start(bf16[192,128]{1,0:T(8,128)(2,1)S(1)} %bitcast.53), channel_id=1, source_target_pairs={{0,2},{1,7},{2,0},{3,5},{4,6},{5,3},{6,4},{7,1},{8,10},{9,15},{10,... | collective-permute-start | bytes 147464 | tf_op jit(solution)/shard_map/ppermute | solution.py:361
  69.1 3.6 %collective-permute-start.6 = (f32[192,512]{1,0:T(8,128)S(1)}, f32[192,512]{1,0:T(8,128)S(1)}, u32[]{:S(2)}, u32[]{:S(2)}) collective-permute-start(f32[192,512]{1,0:T(8,128)S(1)} %get-tuple-element.28), channel_id=1, source_target_pairs={{0,1},{1,0},{2,3},{3,2},{4,5},{5,4},{6,7},{7,6},{8,9},{9,8},{10,11... | collective-permute-start | bytes 1179656 | tf_op jit(solution)/shard_map/ppermute | solution.py:353
  73.2 3.4 %collective-permute-start.7 = (bf16[192,640]{1,0:T(8,128)(2,1)S(1)}, bf16[192,640]{1,0:T(8,128)(2,1)S(1)}, u32[]{:S(2)}, u32[]{:S(2)}) collective-permute-start(bf16[192,640]{1,0:T(8,128)(2,1)S(1)} %get-tuple-element.32.own_ref), channel_id=1, source_target_pairs={{0,1},{1,0},{2,3},{3,2},{4,5},{5,4},{6,7},{7,6},{8,9},{9,8},{10,11... | collective-permute-start | bytes 737288 | tf_op jit(solution)/shard_map/ppermute | solution.py:353
  83.2 7.0 %copy-start.4 = (s32[8,2]{0,1:T(2,128)S(1)}, s32[8,2]{0,1:T(2,128)}, u32[]{:S(2)}) copy-start(s32[8,2]{0,1:T(2,128)} %param.7) | copy-start | bytes 196
  83.2 7.6 %copy-start.5 = (f32[8,8]{1,0:T(8,128)S(1)}, f32[8,8]{1,0:T(8,128)}, u32[]{:S(2)}) copy-start(f32[8,8]{1,0:T(8,128)} %get-tuple-element.35) | copy-start | bytes 772
  83.2 25.7 %all-to-all-start.2 = ((bf16[16,56,768]{2,1,0:T(8,128)(2,1)}), bf16[16,56,768]{2,1,0:T(8,128)(2,1)S(1)}, u32[]{:S(2)}, u32[]{:S(2)}) async-start(bf16[16,56,768]{2,1,0:T(8,128)(2,1)} %shard_map.92), calls=%async_computation.2 | async-start | bytes 2752512 | tf_op jit(solution)/shard_map/all_to_all | solution.py:345
  91.2 18.9 %collective-permute-start.8 = (bf16[192,128]{1,0:T(8,128)(2,1)S(1)}, bf16[192,128]{1,0:T(8,128)(2,1)S(1)}, u32[]{:S(2)}, u32[]{:S(2)}) collective-permute-start(bf16[192,128]{1,0:T(8,128)(2,1)S(1)} %get-tuple-element.34), channel_id=1, source_target_pairs={{0,2},{1,7},{2,0},{3,5},{4,6},{5,3},{6,4},{7,1},{8,10},{9,15},{10,... | collective-permute-start | bytes 147464 | tf_op jit(solution)/shard_map/ppermute | solution.py:361
  110.1 29.6 %all-to-all-start.3 = ((bf16[16,8,512]{2,1,0:T(8,128)(2,1)}), bf16[16,8,512]{2,1,0:T(8,128)(2,1)S(1)}, u32[]{:S(2)}, u32[]{:S(2)}) async-start(bf16[16,8,512]{2,1,0:T(8,128)(2,1)} %bitcast.14), calls=%async_computation.3 | async-start | bytes 262144 | tf_op jit(solution)/shard_map/all_to_all | solution.py:345
  140.9 10.6 %all-to-all-start.4 = ((f32[16,2,768]{2,1,0:T(2,128)}), f32[16,2,768]{2,1,0:T(2,128)S(1)}, u32[]{:S(2)}, u32[]{:S(2)}) async-start(f32[16,2,768]{2,1,0:T(2,128)} %shard_map.94), calls=%async_computation.4 | async-start | bytes 196608 | tf_op jit(solution)/shard_map/all_to_all | solution.py:345
  152.4 9.8 %all-to-all-start.5 = ((bf16[4,24,1536]{2,1,0:T(8,128)(2,1)}), bf16[4,24,1536]{2,1,0:T(8,128)(2,1)S(1)}, u32[]{:S(2)}, u32[]{:S(2)}) async-start(bf16[4,24,1536]{2,1,0:T(8,128)(2,1)} %shard_map.95), calls=%async_computation.5 | async-start | bytes 589824 | tf_op jit(solution)/shard_map/all_to_all | solution.py:345

commit v5 on v4

--- a/solution.py
+++ b/solution.py
@@ -403,7 +403,7 @@
             cost_estimate=cost,
         )(place, *parts)
 
-    near_other = other_half([w_gate, w_up])
+    near_other = other_half([in_hbm(w_gate), in_hbm(w_up)])
     weights = (w_gate, w_up, far_gate, far_up, swap(near_other))
     weights += (swap(other_half([far_gate], LONG)), swap(other_half([far_up], LESS)))
 

time: 164 us -> 164 us (level)
  local copies, waits for them, and re-layouts: 4.92 us -> 2.12 us
    unnamed x19 -> x15, local copies, waits for them, and re-layouts: 3.34 us -> 0.54 us
  transfers between devices with their start and end apart: 15 -> 15, of which waited for: 8 -> 8; matrix products, arithmetic and copies ran while one was open for 2% -> 2% of each run, Pallas kernels for 5% -> 6%
where the time goes in v5:
time: 164 us; the launch traced here: 163 us
  starting transfers between devices  77.4 us (47%)
  waiting for transfers between devices  56.6 us (35%)
  Pallas kernels  22.9 us (14%)
  other arithmetic  2.4 us (1%)
  local copies, waits for them, and re-layouts  2.12 us (1%)
    all_to_all x6, starting transfers between devices, a2a(): return lax.all_to_all(v, axes, split_axis=0, concat_axis=0, tiled=True)  50.1 us
    all_to_all x6, waiting for transfers between devices, a2a(): return lax.all_to_all(v, axes, split_axis=0, concat_axis=0, tiled=True)  46 us
    ppermute x4, starting transfers between devices, along_x(): return lax.ppermute(v, ('xh', 'xl', 'core'), order)  16.3 us
    ppermute x5, starting transfers between devices, swap(): return lax.ppermute(v, 'core', [(0, 1), (1, 0)])  10.9 us
    ppermute x4, waiting for transfers between devices, along_x(): return lax.ppermute(v, ('xh', 'xl', 'core'), order)  8.17 us
    pallas_call x1, Pallas kernels, local(): placed(dx_kernel, (Y,), [whole(slots, 640)] * 2 + [whole(slots, 128)] + w...  6.61 us
    pallas_call x3, Pallas kernels, other_half(): pl.pallas_call(half_kernel, grid_spec=pltpu.PrefetchScalarGridSpec(num_sc...  4.83 us
    pallas_call x1, Pallas kernels, local(): placed(pre_kernel, (1,), [whole(Y * M, BLOCK, piece)] + w_specs(half, 1),...  4.18 us
  transfers between devices with their start and end apart: 15, of which 8 were waited for; matrix products, arithmetic and copies ran while one was open for 2% of the time, Pallas kernels for 6%

profile of v5, /device:TPU:1, one launch (start us, length us, event | category | flops | bytes accessed | tf_op | source)
XLA Modules:
  0.0 162.9 jit_solution(2612549612661765549)
XLA Ops:
  0.6 5.2 %collective-permute-start.1 = (bf16[6144,128]{1,0:T(8,128)(2,1)}, bf16[6144,128]{1,0:T(8,128)(2,1)S(1)}, u32[]{:S(2)}, u32[]{:S(2)}) collective-permute-start(bf16[6144,128]{1,0:T(8,128)(2,1)} %refs_0_.5), channel_id=1, source_target_pairs={{0,2},{1,7},{2,0},{3,5},{4,6},{5,3},{6,4},{7,1},{8,10},{9,15},{10,... | collective-permute-start | bytes 4718600 | tf_op jit(solution)/shard_map/ppermute | solution.py:361
  5.9 2.1 %shard_map.85 = (bf16[8,2,4,768]{3,2,1,0:T(4,128)(2,1)}, f32[8,8]{1,0:T(8,128)}) custom-call(s32[1]{0:T(128)} %bitcast.2.place_ref, s32[2,8]{1,0:T(2,128)} %bitcast.54, bf16[8,6144]{1,0:T(8,128)(2,1)} %tokens_ref.1, bf16[8,6144]{1,0:T(8,128)(2,1)} %bitcast.50), custom_call_target="tpu_custom_call" | custom-call | tf_op jit(solution)/shard_map/pallas_call | solution.py:379
  7.9 15.2 %all-to-all-start = ((bf16[16,4,768]{2,1,0:T(4,128)(2,1)}), bf16[16,4,768]{2,1,0:T(4,128)(2,1)S(1)}, u32[]{:S(2)}, u32[]{:S(2)}) async-start(bf16[16,4,768]{2,1,0:T(4,128)(2,1)} %bitcast.52), calls=%async_computation | async-start | bytes 196608 | tf_op jit(solution)/shard_map/all_to_all | solution.py:345
  23.2 3.3 %collective-permute-start.2 = (bf16[6144,128]{1,0:T(8,128)(2,1)}, bf16[6144,128]{1,0:T(8,128)(2,1)}, u32[]{:S(2)}, u32[]{:S(2)}) collective-permute-start(bf16[6144,128]{1,0:T(8,128)(2,1)} %refs_1_.5), channel_id=1, source_target_pairs={{0,2},{1,7},{2,0},{3,5},{4,6},{5,3},{6,4},{7,1},{8,10},{9,15},{10,... | collective-permute-start | bytes 4718600 | tf_op jit(solution)/shard_map/ppermute | solution.py:361
  26.5 2.6 %shard_map.87 = bf16[2,3072,128]{2,1,0:T(8,128)(2,1)} custom-call(s32[1]{0:T(128)} %bitcast.1.place_ref, bf16[6144,128]{1,0:T(8,128)(2,1)} %refs_0_.5, bf16[6144,128]{1,0:T(8,128)(2,1)} %refs_1_.5), custom_call_target="tpu_custom_call" | custom-call | tf_op jit(solution)/shard_map/pallas_call | solution.py:393
  29.1 1.9 %collective-permute-start.3 = (bf16[2,3072,128]{2,1,0:T(8,128)(2,1)}, bf16[2,3072,128]{2,1,0:T(8,128)(2,1)}, u32[]{:S(2)}, u32[]{:S(2)}) collective-permute-start(bf16[2,3072,128]{2,1,0:T(8,128)(2,1)} %shard_map.87), channel_id=1, source_target_pairs={{0,1},{1,0},{2,3},{3,2},{4,5},{5,4},{6,7},{7,6},{8,9},{9,8},{10,11... | collective-permute-start | bytes 4718600 | tf_op jit(solution)/shard_map/ppermute | solution.py:353
  31.0 6.7 %all-to-all-done.arrived_ref = bf16[16,4,768]{2,1,0:T(4,128)(2,1)S(1)} async-done(((bf16[16,4,768]{2,1,0:T(4,128)(2,1)}), bf16[16,4,768]{2,1,0:T(4,128)(2,1)S(1)}, u32[]{:S(2)}, u32[]{:S(2)}) %all-to-all-start) | async-done | bytes 98336 | tf_op jit(solution)/shard_map/all_to_all | solution.py:345
  37.7 1.4 shard_map.86
  39.1 6.0 %all-to-all-start.1 = ((bf16[16,56,768]{2,1,0:T(8,128)(2,1)}), bf16[16,56,768]{2,1,0:T(8,128)(2,1)S(1)}, u32[]{:S(2)}, u32[]{:S(2)}) async-start(bf16[16,56,768]{2,1,0:T(8,128)(2,1)} %shard_map.86), calls=%async_computation.1 | async-start | bytes 2752512 | tf_op jit(solution)/shard_map/all_to_all | solution.py:345
  45.2 1.0 shard_map.88
  46.6 2.0 %collective-permute-start.4 = (bf16[1,3072,128]{2,1,0:T(8,128)(2,1)}, bf16[1,3072,128]{2,1,0:T(8,128)(2,1)}, u32[]{:S(2)}, u32[]{:S(2)}) collective-permute-start(bf16[1,3072,128]{2,1,0:T(8,128)(2,1)} %shard_map.88), channel_id=1, source_target_pairs={{0,1},{1,0},{2,3},{3,2},{4,5},{5,4},{6,7},{7,6},{8,9},{9,8},{10,11... | collective-permute-start | bytes 2359304 | tf_op jit(solution)/shard_map/ppermute | solution.py:353
  48.6 1.2 shard_map.89
  49.8 2.4 %collective-permute-start.5 = (bf16[1,3072,128]{2,1,0:T(8,128)(2,1)S(1)}, bf16[1,3072,128]{2,1,0:T(8,128)(2,1)}, u32[]{:S(2)}, u32[]{:S(2)}) collective-permute-start(bf16[1,3072,128]{2,1,0:T(8,128)(2,1)S(1)} %shard_map.89), channel_id=1, source_target_pairs={{0,1},{1,0},{2,3},{3,2},{4,5},{5,4},{6,7},{7,6},{8,9},{9,8},{10,11... | collective-permute-start | bytes 2359304 | tf_op jit(solution)/shard_map/ppermute | solution.py:353
  52.6 4.1 %collective-permute-start = (bf16[192,128]{1,0:T(8,128)(2,1)S(1)}, bf16[192,128]{1,0:T(8,128)(2,1)S(1)}, u32[]{:S(2)}, u32[]{:S(2)}) collective-permute-start(bf16[192,128]{1,0:T(8,128)(2,1)S(1)} %bitcast.53), channel_id=1, source_target_pairs={{0,2},{1,7},{2,0},{3,5},{4,6},{5,3},{6,4},{7,1},{8,10},{9,15},{10,... | collective-permute-start | bytes 147464 | tf_op jit(solution)/shard_map/ppermute | solution.py:361
  56.8 8.2 %collective-permute-done.far_cot_ref = bf16[192,128]{1,0:T(8,128)(2,1)S(1)} collective-permute-done((bf16[192,128]{1,0:T(8,128)(2,1)S(1)}, bf16[192,128]{1,0:T(8,128)(2,1)S(1)}, u32[]{:S(2)}, u32[]{:S(2)}) %collective-permute-start) | collective-permute-done | bytes 49184 | tf_op jit(solution)/shard_map/ppermute | solution.py:361
  65.0 4.2 %shard_map.90 = (f32[192,512]{1,0:T(8,128)S(1)}, f32[192,512]{1,0:T(8,128)S(1)}) custom-call(s32[1]{0:T(128)} %bitcast.1.place_ref, bf16[16,56,768]{2,1,0:T(8,128)(2,1)S(1)} %all-to-all-done.1.rows_ref.refs_7_, bf16[6144,128]{1,0:T(8,128)(2,1)} %refs_0_.5, bf16[6144,128]{1,0:T(8,128)(2,1)} %refs_1_.5, bf16[6144,128]{1,0:T(8,128)(2,1)} %copy-done, ...), custom_call_target="tpu_custom_call" | custom-call | tf_op jit(solution)/shard_map/pallas_call | solution.py:436
  69.2 2.3 %collective-permute-start.6 = (f32[192,512]{1,0:T(8,128)S(1)}, f32[192,512]{1,0:T(8,128)S(1)}, u32[]{:S(2)}, u32[]{:S(2)}) collective-permute-start(f32[192,512]{1,0:T(8,128)S(1)} %get-tuple-element.28), channel_id=1, source_target_pairs={{0,1},{1,0},{2,3},{3,2},{4,5},{5,4},{6,7},{7,6},{8,9},{9,8},{10,11... | collective-permute-start | bytes 1179656 | tf_op jit(solution)/shard_map/ppermute | solution.py:353
  71.5 1.3 collective-permute-done.6.core_ref
  73.2 2.3 %collective-permute-start.7 = (bf16[192,640]{1,0:T(8,128)(2,1)S(1)}, bf16[192,640]{1,0:T(8,128)(2,1)S(1)}, u32[]{:S(2)}, u32[]{:S(2)}) collective-permute-start(bf16[192,640]{1,0:T(8,128)(2,1)S(1)} %get-tuple-element.32.own_ref), channel_id=1, source_target_pairs={{0,1},{1,0},{2,3},{3,2},{4,5},{5,4},{6,7},{7,6},{8,9},{9,8},{10,11... | collective-permute-start | bytes 737288 | tf_op jit(solution)/shard_map/ppermute | solution.py:353
  75.5 1.1 collective-permute-done.7.core_ref
  76.6 6.6 %shard_map.92 = bf16[16,56,768]{2,1,0:T(8,128)(2,1)} custom-call(s32[1]{0:T(128)} %bitcast.1.place_ref, bf16[192,640]{1,0:T(8,128)(2,1)S(1)} %get-tuple-element.32.own_ref, bf16[192,640]{1,0:T(8,128)(2,1)S(1)} %collective-permute-done.7.core_ref, f32[192,128]{1,0:T(8,128)S(1)} %get-tuple-element.33.coef_ref, bf16[6144,128]{1,0:T(8,128)(2,1)} %refs_0_.5, ...), custom_call_target="tpu_custom_call" | custom-call | tf_op jit(solution)/shard_map/pallas_call | solution.py:455
  83.2 7.0 %all-to-all-start.2 = ((bf16[16,56,768]{2,1,0:T(8,128)(2,1)}), bf16[16,56,768]{2,1,0:T(8,128)(2,1)S(1)}, u32[]{:S(2)}, u32[]{:S(2)}) async-start(bf16[16,56,768]{2,1,0:T(8,128)(2,1)} %shard_map.92), calls=%async_computation.2 | async-start | bytes 2752512 | tf_op jit(solution)/shard_map/all_to_all | solution.py:345
  91.2 3.6 %collective-permute-start.8 = (bf16[192,128]{1,0:T(8,128)(2,1)S(1)}, bf16[192,128]{1,0:T(8,128)(2,1)S(1)}, u32[]{:S(2)}, u32[]{:S(2)}) collective-permute-start(bf16[192,128]{1,0:T(8,128)(2,1)S(1)} %get-tuple-element.34), channel_id=1, source_target_pairs={{0,2},{1,7},{2,0},{3,5},{4,6},{5,3},{6,4},{7,1},{8,10},{9,15},{10,... | collective-permute-start | bytes 147464 | tf_op jit(solution)/shard_map/ppermute | solution.py:361
  95.7 13.1 %all-to-all-done.2.recv_ref = bf16[16,56,768]{2,1,0:T(8,128)(2,1)S(1)} async-done(((bf16[16,56,768]{2,1,0:T(8,128)(2,1)}), bf16[16,56,768]{2,1,0:T(8,128)(2,1)S(1)}, u32[]{:S(2)}, u32[]{:S(2)}) %all-to-all-start.2) | async-done | bytes 1376288 | tf_op jit(solution)/shard_map/all_to_all | solution.py:345
  108.9 1.2 shard_map.93
  110.1 13.9 %all-to-all-start.3 = ((bf16[16,8,512]{2,1,0:T(8,128)(2,1)}), bf16[16,8,512]{2,1,0:T(8,128)(2,1)S(1)}, u32[]{:S(2)}, u32[]{:S(2)}) async-start(bf16[16,8,512]{2,1,0:T(8,128)(2,1)} %bitcast.14), calls=%async_computation.3 | async-start | bytes 262144 | tf_op jit(solution)/shard_map/all_to_all | solution.py:345
  124.5 15.3 %all-to-all-done.3.home_ref = bf16[16,8,512]{2,1,0:T(8,128)(2,1)S(1)} async-done(((bf16[16,8,512]{2,1,0:T(8,128)(2,1)}), bf16[16,8,512]{2,1,0:T(8,128)(2,1)S(1)}, u32[]{:S(2)}, u32[]{:S(2)}) %all-to-all-start.3) | async-done | bytes 131104 | tf_op jit(solution)/shard_map/all_to_all | solution.py:345
  141.1 4.5 %all-to-all-start.4 = ((f32[16,2,768]{2,1,0:T(2,128)}), f32[16,2,768]{2,1,0:T(2,128)S(1)}, u32[]{:S(2)}, u32[]{:S(2)}) async-start(f32[16,2,768]{2,1,0:T(2,128)} %shard_map.94), calls=%async_computation.4 | async-start | bytes 196608 | tf_op jit(solution)/shard_map/all_to_all | solution.py:345
  146.3 5.3 %all-to-all-done.4.router_ref = f32[16,2,768]{2,1,0:T(2,128)S(1)} async-done(((f32[16,2,768]{2,1,0:T(2,128)}), f32[16,2,768]{2,1,0:T(2,128)S(1)}, u32[]{:S(2)}, u32[]{:S(2)}) %all-to-all-start.4) | async-done | bytes 98336 | tf_op jit(solution)/shard_map/all_to_all | solution.py:345
  151.6 0.8 shard_map.95
  152.4 3.5 %all-to-all-start.5 = ((bf16[4,24,1536]{2,1,0:T(8,128)(2,1)}), bf16[4,24,1536]{2,1,0:T(8,128)(2,1)S(1)}, u32[]{:S(2)}, u32[]{:S(2)}) async-start(bf16[4,24,1536]{2,1,0:T(8,128)(2,1)} %shard_map.95), calls=%async_computation.5 | async-start | bytes 589824 | tf_op jit(solution)/shard_map/all_to_all | solution.py:345
  156.6 5.5 %all-to-all-done.5.got_ref = bf16[4,24,1536]{2,1,0:T(8,128)(2,1)S(1)} async-done(((bf16[4,24,1536]{2,1,0:T(8,128)(2,1)}), bf16[4,24,1536]{2,1,0:T(8,128)(2,1)S(1)}, u32[]{:S(2)}, u32[]{:S(2)}) %all-to-all-start.5) | async-done | bytes 294944 | tf_op jit(solution)/shard_map/all_to_all | solution.py:345
  (71 shorter events, 6.8 us)
Async XLA Ops:
  0.6 44.5 %collective-permute-start.1 = (bf16[6144,128]{1,0:T(8,128)(2,1)}, bf16[6144,128]{1,0:T(8,128)(2,1)S(1)}, u32[]{:S(2)}, u32[]{:S(2)}) collective-permute-start(bf16[6144,128]{1,0:T(8,128)(2,1)} %refs_0_.5), channel_id=1, source_target_pairs={{0,2},{1,7},{2,0},{3,5},{4,6},{5,3},{6,4},{7,1},{8,10},{9,15},{10,... | collective-permute-start | bytes 4718600 | tf_op jit(solution)/shard_map/ppermute | solution.py:361
  7.9 29.8 %all-to-all-start = ((bf16[16,4,768]{2,1,0:T(4,128)(2,1)}), bf16[16,4,768]{2,1,0:T(4,128)(2,1)S(1)}, u32[]{:S(2)}, u32[]{:S(2)}) async-start(bf16[16,4,768]{2,1,0:T(4,128)(2,1)} %bitcast.52), calls=%async_computation | async-start | bytes 196608 | tf_op jit(solution)/shard_map/all_to_all | solution.py:345
  23.2 25.4 %collective-permute-start.2 = (bf16[6144,128]{1,0:T(8,128)(2,1)}, bf16[6144,128]{1,0:T(8,128)(2,1)}, u32[]{:S(2)}, u32[]{:S(2)}) collective-permute-start(bf16[6144,128]{1,0:T(8,128)(2,1)} %refs_1_.5), channel_id=1, source_target_pairs={{0,2},{1,7},{2,0},{3,5},{4,6},{5,3},{6,4},{7,1},{8,10},{9,15},{10,... | collective-permute-start | bytes 4718600 | tf_op jit(solution)/shard_map/ppermute | solution.py:361
  29.1 35.9 %collective-permute-start.3 = (bf16[2,3072,128]{2,1,0:T(8,128)(2,1)}, bf16[2,3072,128]{2,1,0:T(8,128)(2,1)}, u32[]{:S(2)}, u32[]{:S(2)}) collective-permute-start(bf16[2,3072,128]{2,1,0:T(8,128)(2,1)} %shard_map.87), channel_id=1, source_target_pairs={{0,1},{1,0},{2,3},{3,2},{4,5},{5,4},{6,7},{7,6},{8,9},{9,8},{10,11... | collective-permute-start | bytes 4718600 | tf_op jit(solution)/shard_map/ppermute | solution.py:353
  39.1 25.9 %all-to-all-start.1 = ((bf16[16,56,768]{2,1,0:T(8,128)(2,1)}), bf16[16,56,768]{2,1,0:T(8,128)(2,1)S(1)}, u32[]{:S(2)}, u32[]{:S(2)}) async-start(bf16[16,56,768]{2,1,0:T(8,128)(2,1)} %shard_map.86), calls=%async_computation.1 | async-start | bytes 2752512 | tf_op jit(solution)/shard_map/all_to_all | solution.py:345
  45.1 1.4 copy-start
  46.5 5.7 %copy-start.1 = (bf16[384,128]{1,0:T(8,128)(2,1)S(1)}, bf16[384,128]{1,0:T(8,128)(2,1)}, u32[]{:S(2)}) copy-start(bf16[384,128]{1,0:T(8,128)(2,1)} %param.11) | copy-start | bytes 294916
  46.6 18.4 %collective-permute-start.4 = (bf16[1,3072,128]{2,1,0:T(8,128)(2,1)}, bf16[1,3072,128]{2,1,0:T(8,128)(2,1)}, u32[]{:S(2)}, u32[]{:S(2)}) collective-permute-start(bf16[1,3072,128]{2,1,0:T(8,128)(2,1)} %shard_map.88), channel_id=1, source_target_pairs={{0,1},{1,0},{2,3},{3,2},{4,5},{5,4},{6,7},{7,6},{8,9},{9,8},{10,11... | collective-permute-start | bytes 2359304 | tf_op jit(solution)/shard_map/ppermute | solution.py:353
  49.8 15.2 %collective-permute-start.5 = (bf16[1,3072,128]{2,1,0:T(8,128)(2,1)S(1)}, bf16[1,3072,128]{2,1,0:T(8,128)(2,1)}, u32[]{:S(2)}, u32[]{:S(2)}) collective-permute-start(bf16[1,3072,128]{2,1,0:T(8,128)(2,1)S(1)} %shard_map.89), channel_id=1, source_target_pairs={{0,1},{1,0},{2,3},{3,2},{4,5},{5,4},{6,7},{7,6},{8,9},{9,8},{10,11... | collective-permute-start | bytes 2359304 | tf_op jit(solution)/shard_map/ppermute | solution.py:353
  52.6 12.3 %collective-permute-start = (bf16[192,128]{1,0:T(8,128)(2,1)S(1)}, bf16[192,128]{1,0:T(8,128)(2,1)S(1)}, u32[]{:S(2)}, u32[]{:S(2)}) collective-permute-start(bf16[192,128]{1,0:T(8,128)(2,1)S(1)} %bitcast.53), channel_id=1, source_target_pairs={{0,2},{1,7},{2,0},{3,5},{4,6},{5,3},{6,4},{7,1},{8,10},{9,15},{10,... | collective-permute-start | bytes 147464 | tf_op jit(solution)/shard_map/ppermute | solution.py:361
  69.2 3.6 %collective-permute-start.6 = (f32[192,512]{1,0:T(8,128)S(1)}, f32[192,512]{1,0:T(8,128)S(1)}, u32[]{:S(2)}, u32[]{:S(2)}) collective-permute-start(f32[192,512]{1,0:T(8,128)S(1)} %get-tuple-element.28), channel_id=1, source_target_pairs={{0,1},{1,0},{2,3},{3,2},{4,5},{5,4},{6,7},{7,6},{8,9},{9,8},{10,11... | collective-permute-start | bytes 1179656 | tf_op jit(solution)/shard_map/ppermute | solution.py:353
  73.2 3.4 %collective-permute-start.7 = (bf16[192,640]{1,0:T(8,128)(2,1)S(1)}, bf16[192,640]{1,0:T(8,128)(2,1)S(1)}, u32[]{:S(2)}, u32[]{:S(2)}) collective-permute-start(bf16[192,640]{1,0:T(8,128)(2,1)S(1)} %get-tuple-element.32.own_ref), channel_id=1, source_target_pairs={{0,1},{1,0},{2,3},{3,2},{4,5},{5,4},{6,7},{7,6},{8,9},{9,8},{10,11... | collective-permute-start | bytes 737288 | tf_op jit(solution)/shard_map/ppermute | solution.py:353
  83.2 7.0 %copy-start.2 = (s32[8,2]{0,1:T(2,128)S(1)}, s32[8,2]{0,1:T(2,128)}, u32[]{:S(2)}) copy-start(s32[8,2]{0,1:T(2,128)} %param.7) | copy-start | bytes 196
  83.2 7.6 %copy-start.3 = (f32[8,8]{1,0:T(8,128)S(1)}, f32[8,8]{1,0:T(8,128)}, u32[]{:S(2)}) copy-start(f32[8,8]{1,0:T(8,128)} %get-tuple-element.35) | copy-start | bytes 772
  83.2 25.7 %all-to-all-start.2 = ((bf16[16,56,768]{2,1,0:T(8,128)(2,1)}), bf16[16,56,768]{2,1,0:T(8,128)(2,1)S(1)}, u32[]{:S(2)}, u32[]{:S(2)}) async-start(bf16[16,56,768]{2,1,0:T(8,128)(2,1)} %shard_map.92), calls=%async_computation.2 | async-start | bytes 2752512 | tf_op jit(solution)/shard_map/all_to_all | solution.py:345
  91.2 18.9 %collective-permute-start.8 = (bf16[192,128]{1,0:T(8,128)(2,1)S(1)}, bf16[192,128]{1,0:T(8,128)(2,1)S(1)}, u32[]{:S(2)}, u32[]{:S(2)}) collective-permute-start(bf16[192,128]{1,0:T(8,128)(2,1)S(1)} %get-tuple-element.34), channel_id=1, source_target_pairs={{0,2},{1,7},{2,0},{3,5},{4,6},{5,3},{6,4},{7,1},{8,10},{9,15},{10,... | collective-permute-start | bytes 147464 | tf_op jit(solution)/shard_map/ppermute | solution.py:361
  110.1 29.8 %all-to-all-start.3 = ((bf16[16,8,512]{2,1,0:T(8,128)(2,1)}), bf16[16,8,512]{2,1,0:T(8,128)(2,1)S(1)}, u32[]{:S(2)}, u32[]{:S(2)}) async-start(bf16[16,8,512]{2,1,0:T(8,128)(2,1)} %bitcast.14), calls=%async_computation.3 | async-start | bytes 262144 | tf_op jit(solution)/shard_map/all_to_all | solution.py:345
  141.1 10.4 %all-to-all-start.4 = ((f32[16,2,768]{2,1,0:T(2,128)}), f32[16,2,768]{2,1,0:T(2,128)S(1)}, u32[]{:S(2)}, u32[]{:S(2)}) async-start(f32[16,2,768]{2,1,0:T(2,128)} %shard_map.94), calls=%async_computation.4 | async-start | bytes 196608 | tf_op jit(solution)/shard_map/all_to_all | solution.py:345
  152.4 9.8 %all-to-all-start.5 = ((bf16[4,24,1536]{2,1,0:T(8,128)(2,1)}), bf16[4,24,1536]{2,1,0:T(8,128)(2,1)S(1)}, u32[]{:S(2)}, u32[]{:S(2)}) async-start(bf16[4,24,1536]{2,1,0:T(8,128)(2,1)} %shard_map.95), calls=%async_computation.5 | async-start | bytes 589824 | tf_op jit(solution)/shard_map/all_to_all | solution.py:345
